TPU v7x, 32 devices: a whole 2x2x4 slice. The times are simulated.
32 devices in a mesh: seq: 8 (over y, x, core), head: 4 (over z).
Axes of the slice: x: 2, y: 2, z: 4, core: 2. Of those that a mesh axis runs over, the one named last changes fastest.
Arguments:
- queries: bfloat16 [1024, 4096], P('seq', 'head'), may hold values from -500 to 500
- first_key_rows: bfloat16 [1024, 2048], P('seq', 'head'), may hold values from -6 to 6
- first_value_rows: bfloat16 [1024, 2048], P('seq', 'head'), may hold values from -6 to 6
- second_key_rows: bfloat16 [1024, 2048], P('seq', 'head'), may hold values from -6 to 6
- second_value_rows: bfloat16 [1024, 2048], P('seq', 'head'), may hold values from -6 to 6
- out_weight: bfloat16 [4096, 4096], P('head'), may hold values from -6 to 6
Outputs:
- projected: bfloat16 [1024, 4096], P('seq', 'head')
All inputs are finite; a program needn't handle non-finite values.
Results may differ from a plain program's by a relative error of at most 0.015.
The roundings to bfloat16 on the way count: a program that leaves them out, or rounds other values in their place, can miss the bound.
Values may be sent and summed in bfloat16 or wider, within the bound.
A program may use at most 64 MiB of HBM per device.

v0:
```python
import jax
import jax.numpy as jnp
from jax import lax
from jax.sharding import PartitionSpec as P

HEAD_SIZE = 128
W1 = 512
W2 = 32


def from_behind(shard, axis, by):
    length = lax.axis_size(axis)
    pairs = [(i, i + by) for i in range(length) if 0 <= i + by < length]
    return lax.ppermute(shard, axis, pairs)


def lag_windows(rows, span, count):
    feature_count = rows.shape[1]
    padded = jnp.concatenate([rows, jnp.zeros((1, feature_count), rows.dtype)], axis=0)
    length = padded.shape[0]
    tiled = jnp.broadcast_to(padded[None], (span, length, feature_count)).reshape(
        span * length, feature_count
    )
    return tiled[: span * (length - 1)].reshape(span, length - 1, feature_count)[
        :, span : span + count
    ]


def window_attend(query_block, outer_keys, outer_values, inner_keys, inner_values, first_pos):
    row_count = query_block.shape[0]
    inner_span = inner_keys.shape[0] - row_count
    outer_span = outer_keys.shape[0] - row_count
    scale_factor = query_block.shape[1] ** (-0.5)
    inner_key_win = lag_windows(inner_keys, inner_span, row_count)
    inner_val_win = lag_windows(inner_values, inner_span, row_count)
    blended = (query_block.astype(jnp.float32)[None] * inner_key_win.astype(jnp.float32)).astype(
        jnp.bfloat16
    )
    scores = (
        jnp.einsum("wid,jd->wij", blended, outer_keys, preferred_element_type=jnp.float32)
        * scale_factor
    )
    row_index = lax.broadcasted_iota(jnp.int32, scores.shape, 1)
    col_index = lax.broadcasted_iota(jnp.int32, scores.shape, 2)
    lag_index = lax.broadcasted_iota(jnp.int32, scores.shape, 0)
    allowed = (col_index > row_index) & (col_index <= row_index + outer_span)
    allowed = (
        allowed
        & (first_pos - outer_span + col_index >= 0)
        & (first_pos + row_index - lag_index >= 0)
    )
    scores = jnp.where(allowed, scores, -1e30)
    row_max = jnp.max(scores, axis=(0, 2), keepdims=True)
    expon = jnp.where(allowed, jnp.exp(scores - row_max), 0.0)
    row_total = jnp.sum(expon, axis=(0, 2), keepdims=True)
    weights = (expon / row_total).astype(jnp.bfloat16)
    inner_sum = jnp.einsum("wij,jd->wid", weights, outer_values, preferred_element_type=jnp.float32)
    return jnp.sum(inner_val_win.astype(jnp.float32) * inner_sum, axis=0)


def local(
    queries, first_key_rows, first_value_rows, second_key_rows, second_value_rows, out_weight
):
    row_count = queries.shape[0]
    head_count = queries.shape[1] // HEAD_SIZE
    query_group_width = head_count // (first_key_rows.shape[1] // HEAD_SIZE)
    shard_count = W1 // row_count
    first_pos = lax.axis_index("seq") * row_count
    tail_rows = (second_key_rows[row_count - W2 :], second_value_rows[row_count - W2 :])
    prior_inner = from_behind((tail_rows[0], tail_rows[1]), "seq", 1)
    pieces_keys = []
    pieces_values = []
    for distance in range(shard_count, 0, -1):
        arrived = from_behind((first_key_rows, first_value_rows), "seq", distance)
        pieces_keys.append(arrived[0])
        pieces_values.append(arrived[1])
    prior_keys = jnp.concatenate(pieces_keys, axis=0)
    prior_values = jnp.concatenate(pieces_values, axis=0)
    outer_keys_all = jnp.concatenate([prior_keys, first_key_rows], axis=0)
    outer_vals_all = jnp.concatenate([prior_values, first_value_rows], axis=0)
    inner_keys_all = jnp.concatenate([prior_inner[0], second_key_rows], axis=0)
    inner_vals_all = jnp.concatenate([prior_inner[1], second_value_rows], axis=0)

    def per_head(head):
        kv_start = head // query_group_width * HEAD_SIZE
        return window_attend(
            lax.dynamic_slice_in_dim(queries, head * HEAD_SIZE, HEAD_SIZE, 1),
            lax.dynamic_slice_in_dim(outer_keys_all, kv_start, HEAD_SIZE, 1),
            lax.dynamic_slice_in_dim(outer_vals_all, kv_start, HEAD_SIZE, 1),
            lax.dynamic_slice_in_dim(inner_keys_all, kv_start, HEAD_SIZE, 1),
            lax.dynamic_slice_in_dim(inner_vals_all, kv_start, HEAD_SIZE, 1),
            first_pos,
        ).astype(jnp.bfloat16)

    heads_out = lax.map(per_head, jnp.arange(head_count, dtype=jnp.int32))
    attended = jnp.transpose(heads_out, (1, 0, 2)).reshape(row_count, head_count * HEAD_SIZE)
    shared = lax.psum_scatter(
        lax.dot_general(
            out_weight, attended, (((0,), (1,)), ((), ())), preferred_element_type=jnp.float32
        ).astype(jnp.bfloat16),
        "head",
        scatter_dimension=0,
        tiled=True,
    )
    return jnp.transpose(shared)


def solution(mesh):
    in_specs = (
        P("seq", "head"),
        P("seq", "head"),
        P("seq", "head"),
        P("seq", "head"),
        P("seq", "head"),
        P("head", None),
    )
    out_specs = P("seq", "head")
    return jax.shard_map(local, mesh=mesh, in_specs=in_specs, out_specs=out_specs, check_vma=False)
```

profile of v0, /device:TPU:0, one launch (start us, length us, event | category | flops | bytes accessed | tf_op | source)
XLA Modules:
  0.0 254.1 jit_solution(7655210373429472857)
XLA Ops:
  9.7 4.4 %collective-permute-start.4 = (bf16[128,512]{1,0:T(8,128)(2,1)}, bf16[128,512]{1,0:T(8,128)(2,1)S(1)}, u32[]{:S(2)}, u32[]{:S(2)}) collective-permute-start(bf16[128,512]{1,0:T(8,128)(2,1)} %param.9), channel_id=1, source_target_pairs={{0,8},{4,12},{8,16},{12,20},{16,24},{20,28},{1,9},{5,13},{9,17},{1... | collective-permute-start | bytes 393224 | tf_op jit(solution)/shard_map/ppermute | solution.py:14
  14.1 4.3 %collective-permute-start.3 = (bf16[128,512]{1,0:T(8,128)(2,1)}, bf16[128,512]{1,0:T(8,128)(2,1)S(1)}, u32[]{:S(2)}, u32[]{:S(2)}) collective-permute-start(bf16[128,512]{1,0:T(8,128)(2,1)} %param.9), channel_id=1, source_target_pairs={{0,12},{4,16},{8,20},{12,24},{16,28},{1,13},{5,17},{9,21},{13,25},... | collective-permute-start | bytes 393224 | tf_op jit(solution)/shard_map/ppermute | solution.py:14
  24.4 2.5 collective-permute-start.7
  30.2 2.8 %collective-permute-start.9 = (bf16[128,512]{1,0:T(8,128)(2,1)}, bf16[128,512]{1,0:T(8,128)(2,1)S(1)}, u32[]{:S(2)}, u32[]{:S(2)}) collective-permute-start(bf16[128,512]{1,0:T(8,128)(2,1)} %param.10), channel_id=1, source_target_pairs={{0,4},{4,8},{8,12},{12,16},{16,20},{20,24},{24,28},{1,5},{5,9},{9,... | collective-permute-start | bytes 393224 | tf_op jit(solution)/shard_map/ppermute | solution.py:14
  33.6 3.9 %collective-permute-start.5 = (bf16[128,512]{1,0:T(8,128)(2,1)}, bf16[128,512]{1,0:T(8,128)(2,1)S(1)}, u32[]{:S(2)}, u32[]{:S(2)}) collective-permute-start(bf16[128,512]{1,0:T(8,128)(2,1)} %param.9), channel_id=1, source_target_pairs={{0,4},{4,8},{8,12},{12,16},{16,20},{20,24},{24,28},{1,5},{5,9},{9,... | collective-permute-start | bytes 393224 | tf_op jit(solution)/shard_map/ppermute | solution.py:14
  39.6 168.6 %while.12 = (s32[]{:T(128)}, bf16[8,128,128]{1,2,0:T(8,128)(2,1)S(1)}, s32[8]{0:T(128)S(1)}, bf16[160,512]{1,0:T(8,128)(2,1)S(1)}, s32[]{:T(128)}, /*index=5*/s3...) while((s32[]{:T(128)}, ...), condition=%wide.region_4.5_spmd, body=%wide.region_0.4_spmd.sunk | while | flops 1437074688 | bytes 64859496 | solution.py:95
  48.0 3.9 %fusion.26 = (f32[128]{0:T(128)S(1)}, f32[32,128,640]{2,1,0:T(8,128)S(1)}) fusion(s32[128]{0:T(128)S(1)} %get-tuple-element.220, pred[640]{0:T(1024)(128)(4,1)S(1)} %add_compare_fusion.2, s32[128]{0:T(128)S(1)} %get-tuple-element.221, bf16[640,512]{1,0:T(8,128)(2,1)} %copy-done.3, s32[]{:T(128)S(6)} %select_n.70, ...), kind=kOutput, calls=%fused_computation.9.clone.1 | convolution fusion | flops 698875776 | bytes 11766276 | tf_op jit(solution)/shard_map/while/body/eval_jaxpr/wid,jd->wij/dot_general | solution.py:40
  51.9 4.1 %fusion.27 = f32[128]{0:T(128)S(1)} fusion(f32[32,128,640]{2,1,0:T(8,128)S(1)} %get-tuple-element.223, f32[128]{0:T(128)S(1)} %get-tuple-element.224, s32[128]{0:T(128)S(1)} %get-tuple-element.220, pred[640]{0:T(1024)(128)(4,1)S(1)} %add_compare_fusion.2, s32[128]{0:T(128)S(1)} %get-tuple-element.221), kind=kLoop, calls=%fused_computation.10.clone.1 | loop fusion | flops 31457152 | bytes 10488448 | tf_op jit(solution)/shard_map/while/body/eval_jaxpr/reduce_sum | solution.py:55
  56.0 4.5 %multiply_reduce_fusion.2 = bf16[128,128]{1,0:T(8,128)(2,1)S(1)} fusion(f32[32,128,640]{2,1,0:T(8,128)S(1)} %get-tuple-element.223, f32[128]{0:T(128)S(1)} %fusion.27, f32[128]{0:T(128)S(1)} %get-tuple-element.224, s32[128]{0:T(128)S(1)} %get-tuple-element.220, s32[128]{0:T(128)S(1)} %get-tuple-element.221, ...), kind=kOutput, calls=%fused_computation.12.clone.1 | convolution fusion | flops 706723840 | bytes 11734020 | tf_op jit(solution)/shard_map/while/body/eval_jaxpr/wij,jd->wid/dot_general | solution.py:57
  69.1 3.9 %fusion.26 = (f32[128]{0:T(128)S(1)}, f32[32,128,640]{2,1,0:T(8,128)S(1)}) fusion(s32[128]{0:T(128)S(1)} %get-tuple-element.220, pred[640]{0:T(1024)(128)(4,1)S(1)} %add_compare_fusion.2, s32[128]{0:T(128)S(1)} %get-tuple-element.221, bf16[640,512]{1,0:T(8,128)(2,1)} %copy-done.3, s32[]{:T(128)S(6)} %select_n.70, ...), kind=kOutput, calls=%fused_computation.9.clone.1 | convolution fusion | flops 698875776 | bytes 11766276 | tf_op jit(solution)/shard_map/while/body/eval_jaxpr/wid,jd->wij/dot_general | solution.py:40
  73.0 4.1 %fusion.27 = f32[128]{0:T(128)S(1)} fusion(f32[32,128,640]{2,1,0:T(8,128)S(1)} %get-tuple-element.223, f32[128]{0:T(128)S(1)} %get-tuple-element.224, s32[128]{0:T(128)S(1)} %get-tuple-element.220, pred[640]{0:T(1024)(128)(4,1)S(1)} %add_compare_fusion.2, s32[128]{0:T(128)S(1)} %get-tuple-element.221), kind=kLoop, calls=%fused_computation.10.clone.1 | loop fusion | flops 31457152 | bytes 10488448 | tf_op jit(solution)/shard_map/while/body/eval_jaxpr/reduce_sum | solution.py:55
  77.1 4.5 %multiply_reduce_fusion.2 = bf16[128,128]{1,0:T(8,128)(2,1)S(1)} fusion(f32[32,128,640]{2,1,0:T(8,128)S(1)} %get-tuple-element.223, f32[128]{0:T(128)S(1)} %fusion.27, f32[128]{0:T(128)S(1)} %get-tuple-element.224, s32[128]{0:T(128)S(1)} %get-tuple-element.220, s32[128]{0:T(128)S(1)} %get-tuple-element.221, ...), kind=kOutput, calls=%fused_computation.12.clone.1 | convolution fusion | flops 706723840 | bytes 11734020 | tf_op jit(solution)/shard_map/while/body/eval_jaxpr/wij,jd->wid/dot_general | solution.py:57
  90.1 3.9 %fusion.26 = (f32[128]{0:T(128)S(1)}, f32[32,128,640]{2,1,0:T(8,128)S(1)}) fusion(s32[128]{0:T(128)S(1)} %get-tuple-element.220, pred[640]{0:T(1024)(128)(4,1)S(1)} %add_compare_fusion.2, s32[128]{0:T(128)S(1)} %get-tuple-element.221, bf16[640,512]{1,0:T(8,128)(2,1)} %copy-done.3, s32[]{:T(128)S(6)} %select_n.70, ...), kind=kOutput, calls=%fused_computation.9.clone.1 | convolution fusion | flops 698875776 | bytes 11766276 | tf_op jit(solution)/shard_map/while/body/eval_jaxpr/wid,jd->wij/dot_general | solution.py:40
  94.0 4.1 %fusion.27 = f32[128]{0:T(128)S(1)} fusion(f32[32,128,640]{2,1,0:T(8,128)S(1)} %get-tuple-element.223, f32[128]{0:T(128)S(1)} %get-tuple-element.224, s32[128]{0:T(128)S(1)} %get-tuple-element.220, pred[640]{0:T(1024)(128)(4,1)S(1)} %add_compare_fusion.2, s32[128]{0:T(128)S(1)} %get-tuple-element.221), kind=kLoop, calls=%fused_computation.10.clone.1 | loop fusion | flops 31457152 | bytes 10488448 | tf_op jit(solution)/shard_map/while/body/eval_jaxpr/reduce_sum | solution.py:55
  98.2 4.5 %multiply_reduce_fusion.2 = bf16[128,128]{1,0:T(8,128)(2,1)S(1)} fusion(f32[32,128,640]{2,1,0:T(8,128)S(1)} %get-tuple-element.223, f32[128]{0:T(128)S(1)} %fusion.27, f32[128]{0:T(128)S(1)} %get-tuple-element.224, s32[128]{0:T(128)S(1)} %get-tuple-element.220, s32[128]{0:T(128)S(1)} %get-tuple-element.221, ...), kind=kOutput, calls=%fused_computation.12.clone.1 | convolution fusion | flops 706723840 | bytes 11734020 | tf_op jit(solution)/shard_map/while/body/eval_jaxpr/wij,jd->wid/dot_general | solution.py:57
  111.2 3.9 %fusion.26 = (f32[128]{0:T(128)S(1)}, f32[32,128,640]{2,1,0:T(8,128)S(1)}) fusion(s32[128]{0:T(128)S(1)} %get-tuple-element.220, pred[640]{0:T(1024)(128)(4,1)S(1)} %add_compare_fusion.2, s32[128]{0:T(128)S(1)} %get-tuple-element.221, bf16[640,512]{1,0:T(8,128)(2,1)} %copy-done.3, s32[]{:T(128)S(6)} %select_n.70, ...), kind=kOutput, calls=%fused_computation.9.clone.1 | convolution fusion | flops 698875776 | bytes 11766276 | tf_op jit(solution)/shard_map/while/body/eval_jaxpr/wid,jd->wij/dot_general | solution.py:40
  115.1 4.1 %fusion.27 = f32[128]{0:T(128)S(1)} fusion(f32[32,128,640]{2,1,0:T(8,128)S(1)} %get-tuple-element.223, f32[128]{0:T(128)S(1)} %get-tuple-element.224, s32[128]{0:T(128)S(1)} %get-tuple-element.220, pred[640]{0:T(1024)(128)(4,1)S(1)} %add_compare_fusion.2, s32[128]{0:T(128)S(1)} %get-tuple-element.221), kind=kLoop, calls=%fused_computation.10.clone.1 | loop fusion | flops 31457152 | bytes 10488448 | tf_op jit(solution)/shard_map/while/body/eval_jaxpr/reduce_sum | solution.py:55
  119.3 4.5 %multiply_reduce_fusion.2 = bf16[128,128]{1,0:T(8,128)(2,1)S(1)} fusion(f32[32,128,640]{2,1,0:T(8,128)S(1)} %get-tuple-element.223, f32[128]{0:T(128)S(1)} %fusion.27, f32[128]{0:T(128)S(1)} %get-tuple-element.224, s32[128]{0:T(128)S(1)} %get-tuple-element.220, s32[128]{0:T(128)S(1)} %get-tuple-element.221, ...), kind=kOutput, calls=%fused_computation.12.clone.1 | convolution fusion | flops 706723840 | bytes 11734020 | tf_op jit(solution)/shard_map/while/body/eval_jaxpr/wij,jd->wid/dot_general | solution.py:57
  132.3 3.9 %fusion.26 = (f32[128]{0:T(128)S(1)}, f32[32,128,640]{2,1,0:T(8,128)S(1)}) fusion(s32[128]{0:T(128)S(1)} %get-tuple-element.220, pred[640]{0:T(1024)(128)(4,1)S(1)} %add_compare_fusion.2, s32[128]{0:T(128)S(1)} %get-tuple-element.221, bf16[640,512]{1,0:T(8,128)(2,1)} %copy-done.3, s32[]{:T(128)S(6)} %select_n.70, ...), kind=kOutput, calls=%fused_computation.9.clone.1 | convolution fusion | flops 698875776 | bytes 11766276 | tf_op jit(solution)/shard_map/while/body/eval_jaxpr/wid,jd->wij/dot_general | solution.py:40
  136.2 4.1 %fusion.27 = f32[128]{0:T(128)S(1)} fusion(f32[32,128,640]{2,1,0:T(8,128)S(1)} %get-tuple-element.223, f32[128]{0:T(128)S(1)} %get-tuple-element.224, s32[128]{0:T(128)S(1)} %get-tuple-element.220, pred[640]{0:T(1024)(128)(4,1)S(1)} %add_compare_fusion.2, s32[128]{0:T(128)S(1)} %get-tuple-element.221), kind=kLoop, calls=%fused_computation.10.clone.1 | loop fusion | flops 31457152 | bytes 10488448 | tf_op jit(solution)/shard_map/while/body/eval_jaxpr/reduce_sum | solution.py:55
  140.3 4.5 %multiply_reduce_fusion.2 = bf16[128,128]{1,0:T(8,128)(2,1)S(1)} fusion(f32[32,128,640]{2,1,0:T(8,128)S(1)} %get-tuple-element.223, f32[128]{0:T(128)S(1)} %fusion.27, f32[128]{0:T(128)S(1)} %get-tuple-element.224, s32[128]{0:T(128)S(1)} %get-tuple-element.220, s32[128]{0:T(128)S(1)} %get-tuple-element.221, ...), kind=kOutput, calls=%fused_computation.12.clone.1 | convolution fusion | flops 706723840 | bytes 11734020 | tf_op jit(solution)/shard_map/while/body/eval_jaxpr/wij,jd->wid/dot_general | solution.py:57
  153.4 3.9 %fusion.26 = (f32[128]{0:T(128)S(1)}, f32[32,128,640]{2,1,0:T(8,128)S(1)}) fusion(s32[128]{0:T(128)S(1)} %get-tuple-element.220, pred[640]{0:T(1024)(128)(4,1)S(1)} %add_compare_fusion.2, s32[128]{0:T(128)S(1)} %get-tuple-element.221, bf16[640,512]{1,0:T(8,128)(2,1)} %copy-done.3, s32[]{:T(128)S(6)} %select_n.70, ...), kind=kOutput, calls=%fused_computation.9.clone.1 | convolution fusion | flops 698875776 | bytes 11766276 | tf_op jit(solution)/shard_map/while/body/eval_jaxpr/wid,jd->wij/dot_general | solution.py:40
  157.2 4.1 %fusion.27 = f32[128]{0:T(128)S(1)} fusion(f32[32,128,640]{2,1,0:T(8,128)S(1)} %get-tuple-element.223, f32[128]{0:T(128)S(1)} %get-tuple-element.224, s32[128]{0:T(128)S(1)} %get-tuple-element.220, pred[640]{0:T(1024)(128)(4,1)S(1)} %add_compare_fusion.2, s32[128]{0:T(128)S(1)} %get-tuple-element.221), kind=kLoop, calls=%fused_computation.10.clone.1 | loop fusion | flops 31457152 | bytes 10488448 | tf_op jit(solution)/shard_map/while/body/eval_jaxpr/reduce_sum | solution.py:55
  161.4 4.5 %multiply_reduce_fusion.2 = bf16[128,128]{1,0:T(8,128)(2,1)S(1)} fusion(f32[32,128,640]{2,1,0:T(8,128)S(1)} %get-tuple-element.223, f32[128]{0:T(128)S(1)} %fusion.27, f32[128]{0:T(128)S(1)} %get-tuple-element.224, s32[128]{0:T(128)S(1)} %get-tuple-element.220, s32[128]{0:T(128)S(1)} %get-tuple-element.221, ...), kind=kOutput, calls=%fused_computation.12.clone.1 | convolution fusion | flops 706723840 | bytes 11734020 | tf_op jit(solution)/shard_map/while/body/eval_jaxpr/wij,jd->wid/dot_general | solution.py:57
  174.4 3.9 %fusion.26 = (f32[128]{0:T(128)S(1)}, f32[32,128,640]{2,1,0:T(8,128)S(1)}) fusion(s32[128]{0:T(128)S(1)} %get-tuple-element.220, pred[640]{0:T(1024)(128)(4,1)S(1)} %add_compare_fusion.2, s32[128]{0:T(128)S(1)} %get-tuple-element.221, bf16[640,512]{1,0:T(8,128)(2,1)} %copy-done.3, s32[]{:T(128)S(6)} %select_n.70, ...), kind=kOutput, calls=%fused_computation.9.clone.1 | convolution fusion | flops 698875776 | bytes 11766276 | tf_op jit(solution)/shard_map/while/body/eval_jaxpr/wid,jd->wij/dot_general | solution.py:40
  178.3 4.1 %fusion.27 = f32[128]{0:T(128)S(1)} fusion(f32[32,128,640]{2,1,0:T(8,128)S(1)} %get-tuple-element.223, f32[128]{0:T(128)S(1)} %get-tuple-element.224, s32[128]{0:T(128)S(1)} %get-tuple-element.220, pred[640]{0:T(1024)(128)(4,1)S(1)} %add_compare_fusion.2, s32[128]{0:T(128)S(1)} %get-tuple-element.221), kind=kLoop, calls=%fused_computation.10.clone.1 | loop fusion | flops 31457152 | bytes 10488448 | tf_op jit(solution)/shard_map/while/body/eval_jaxpr/reduce_sum | solution.py:55
  182.5 4.5 %multiply_reduce_fusion.2 = bf16[128,128]{1,0:T(8,128)(2,1)S(1)} fusion(f32[32,128,640]{2,1,0:T(8,128)S(1)} %get-tuple-element.223, f32[128]{0:T(128)S(1)} %fusion.27, f32[128]{0:T(128)S(1)} %get-tuple-element.224, s32[128]{0:T(128)S(1)} %get-tuple-element.220, s32[128]{0:T(128)S(1)} %get-tuple-element.221, ...), kind=kOutput, calls=%fused_computation.12.clone.1 | convolution fusion | flops 706723840 | bytes 11734020 | tf_op jit(solution)/shard_map/while/body/eval_jaxpr/wij,jd->wid/dot_general | solution.py:57
  195.5 3.8 %fusion.26 = (f32[128]{0:T(128)S(1)}, f32[32,128,640]{2,1,0:T(8,128)S(1)}) fusion(s32[128]{0:T(128)S(1)} %get-tuple-element.220, pred[640]{0:T(1024)(128)(4,1)S(1)} %add_compare_fusion.2, s32[128]{0:T(128)S(1)} %get-tuple-element.221, bf16[640,512]{1,0:T(8,128)(2,1)} %copy-done.3, s32[]{:T(128)S(6)} %select_n.70, ...), kind=kOutput, calls=%fused_computation.9.clone.1 | convolution fusion | flops 698875776 | bytes 11766276 | tf_op jit(solution)/shard_map/while/body/eval_jaxpr/wid,jd->wij/dot_general | solution.py:40
  199.4 4.1 %fusion.27 = f32[128]{0:T(128)S(1)} fusion(f32[32,128,640]{2,1,0:T(8,128)S(1)} %get-tuple-element.223, f32[128]{0:T(128)S(1)} %get-tuple-element.224, s32[128]{0:T(128)S(1)} %get-tuple-element.220, pred[640]{0:T(1024)(128)(4,1)S(1)} %add_compare_fusion.2, s32[128]{0:T(128)S(1)} %get-tuple-element.221), kind=kLoop, calls=%fused_computation.10.clone.1 | loop fusion | flops 31457152 | bytes 10488448 | tf_op jit(solution)/shard_map/while/body/eval_jaxpr/reduce_sum | solution.py:55
  203.6 4.5 %multiply_reduce_fusion.2 = bf16[128,128]{1,0:T(8,128)(2,1)S(1)} fusion(f32[32,128,640]{2,1,0:T(8,128)S(1)} %get-tuple-element.223, f32[128]{0:T(128)S(1)} %fusion.27, f32[128]{0:T(128)S(1)} %get-tuple-element.224, s32[128]{0:T(128)S(1)} %get-tuple-element.220, s32[128]{0:T(128)S(1)} %get-tuple-element.221, ...), kind=kOutput, calls=%fused_computation.12.clone.1 | convolution fusion | flops 706723840 | bytes 11734020 | tf_op jit(solution)/shard_map/while/body/eval_jaxpr/wij,jd->wid/dot_general | solution.py:57
  208.2 5.7 %fusion.19 = bf16[4096,128]{0,1:T(8,128)(2,1)} fusion(bf16[128,1024]{0,1:T(8,128)(2,1)S(1)} %bitcast.37, bf16[1024,4096]{1,0:T(8,128)(2,1)} %param.13), kind=kOutput, calls=%fused_computation.35 | convolution fusion | flops 1074266112 | bytes 9699328 | tf_op jit(solution)/shard_map/dot_general | solution.py:98
  213.9 33.4 %reduce-scatter.2.cloned.1.call-done = bf16[1024,128]{0,1:T(8,128)(2,1)} async-done(((bf16[4096,128]{0,1:T(8,128)(2,1)}), bf16[1024,128]{0,1:T(8,128)(2,1)}) %reduce-scatter.2.cloned.1.call-update) | async-done | bytes 262160 | tf_op jit(solution)/shard_map/reduce_scatter | solution.py:97
  (241 shorter events, 56.8 us)
Async XLA Ops:
  6.5 240.8 %reduce-scatter.2.cloned.1.call-start = ((), (), s32[]{:S(2)}) async-start(), calls=%async_computation.1 | async-start | bytes 1310720 | tf_op jit(solution)/shard_map/reduce_scatter | solution.py:97
  7.3 14.5 %collective-permute-start.1 = (bf16[32,512]{1,0:T(8,128)(2,1)S(1)}, bf16[32,512]{1,0:T(8,128)(2,1)S(1)}, u32[]{:S(2)}, u32[]{:S(2)}) collective-permute-start(bf16[32,512]{1,0:T(8,128)(2,1)S(1)} %slice.31), channel_id=1, source_target_pairs={{0,4},{4,8},{8,12},{12,16},{16,20},{20,24},{24,28},{1,5},{5,9},{9,... | collective-permute-start | bytes 98312 | tf_op jit(solution)/shard_map/ppermute | solution.py:14
  9.7 28.8 %collective-permute-start.4 = (bf16[128,512]{1,0:T(8,128)(2,1)}, bf16[128,512]{1,0:T(8,128)(2,1)S(1)}, u32[]{:S(2)}, u32[]{:S(2)}) collective-permute-start(bf16[128,512]{1,0:T(8,128)(2,1)} %param.9), channel_id=1, source_target_pairs={{0,8},{4,12},{8,16},{12,20},{16,24},{20,28},{1,9},{5,13},{9,17},{1... | collective-permute-start | bytes 393224 | tf_op jit(solution)/shard_map/ppermute | solution.py:14
  14.1 24.4 %collective-permute-start.3 = (bf16[128,512]{1,0:T(8,128)(2,1)}, bf16[128,512]{1,0:T(8,128)(2,1)S(1)}, u32[]{:S(2)}, u32[]{:S(2)}) collective-permute-start(bf16[128,512]{1,0:T(8,128)(2,1)} %param.9), channel_id=1, source_target_pairs={{0,12},{4,16},{8,20},{12,24},{16,28},{1,13},{5,17},{9,21},{13,25},... | collective-permute-start | bytes 393224 | tf_op jit(solution)/shard_map/ppermute | solution.py:14
  18.4 20.0 %collective-permute-start.2 = (bf16[128,512]{1,0:T(8,128)(2,1)}, bf16[128,512]{1,0:T(8,128)(2,1)S(1)}, u32[]{:S(2)}, u32[]{:S(2)}) collective-permute-start(bf16[128,512]{1,0:T(8,128)(2,1)} %param.9), channel_id=1, source_target_pairs={{0,16},{4,20},{8,24},{12,28},{1,17},{5,21},{9,25},{13,29},{2,18},{... | collective-permute-start | bytes 393224 | tf_op jit(solution)/shard_map/ppermute | solution.py:14
  20.5 3.9 %collective-permute-start = (bf16[32,512]{1,0:T(8,128)(2,1)S(1)}, bf16[32,512]{1,0:T(8,128)(2,1)S(1)}, u32[]{:S(2)}, u32[]{:S(2)}) collective-permute-start(bf16[32,512]{1,0:T(8,128)(2,1)S(1)} %slice.30), channel_id=1, source_target_pairs={{0,4},{4,8},{8,12},{12,16},{16,20},{20,24},{24,28},{1,5},{5,9},{9,... | collective-permute-start | bytes 98312 | tf_op jit(solution)/shard_map/ppermute | solution.py:14
  21.8 6.0 %collective-permute-start.6 = (bf16[128,512]{1,0:T(8,128)(2,1)}, bf16[128,512]{1,0:T(8,128)(2,1)S(1)}, u32[]{:S(2)}, u32[]{:S(2)}) collective-permute-start(bf16[128,512]{1,0:T(8,128)(2,1)} %param.10), channel_id=1, source_target_pairs={{0,16},{4,20},{8,24},{12,28},{1,17},{5,21},{9,25},{13,29},{2,18},{... | collective-permute-start | bytes 393224 | tf_op jit(solution)/shard_map/ppermute | solution.py:14
  24.4 5.8 %collective-permute-start.7 = (bf16[128,512]{1,0:T(8,128)(2,1)}, bf16[128,512]{1,0:T(8,128)(2,1)S(1)}, u32[]{:S(2)}, u32[]{:S(2)}) collective-permute-start(bf16[128,512]{1,0:T(8,128)(2,1)} %param.10), channel_id=1, source_target_pairs={{0,12},{4,16},{8,20},{12,24},{16,28},{1,13},{5,17},{9,21},{13,25},... | collective-permute-start | bytes 393224 | tf_op jit(solution)/shard_map/ppermute | solution.py:14
  27.8 5.8 %collective-permute-start.8 = (bf16[128,512]{1,0:T(8,128)(2,1)}, bf16[128,512]{1,0:T(8,128)(2,1)S(1)}, u32[]{:S(2)}, u32[]{:S(2)}) collective-permute-start(bf16[128,512]{1,0:T(8,128)(2,1)} %param.10), channel_id=1, source_target_pairs={{0,8},{4,12},{8,16},{12,20},{16,24},{20,28},{1,9},{5,13},{9,17},{1... | collective-permute-start | bytes 393224 | tf_op jit(solution)/shard_map/ppermute | solution.py:14
  30.2 7.3 %collective-permute-start.9 = (bf16[128,512]{1,0:T(8,128)(2,1)}, bf16[128,512]{1,0:T(8,128)(2,1)S(1)}, u32[]{:S(2)}, u32[]{:S(2)}) collective-permute-start(bf16[128,512]{1,0:T(8,128)(2,1)} %param.10), channel_id=1, source_target_pairs={{0,4},{4,8},{8,12},{12,16},{16,20},{20,24},{24,28},{1,5},{5,9},{9,... | collective-permute-start | bytes 393224 | tf_op jit(solution)/shard_map/ppermute | solution.py:14
  33.6 5.1 %collective-permute-start.5 = (bf16[128,512]{1,0:T(8,128)(2,1)}, bf16[128,512]{1,0:T(8,128)(2,1)S(1)}, u32[]{:S(2)}, u32[]{:S(2)}) collective-permute-start(bf16[128,512]{1,0:T(8,128)(2,1)} %param.9), channel_id=1, source_target_pairs={{0,4},{4,8},{8,12},{12,16},{16,20},{20,24},{24,28},{1,5},{5,9},{9,... | collective-permute-start | bytes 393224 | tf_op jit(solution)/shard_map/ppermute | solution.py:14
  39.6 4.8 %copy-start.3 = (bf16[640,512]{1,0:T(8,128)(2,1)}, bf16[640,512]{1,0:T(8,128)(2,1)S(1)}, u32[]{:S(2)}) copy-start(bf16[640,512]{1,0:T(8,128)(2,1)S(1)} %get-tuple-element.268) | copy-start | bytes 1966084 | tf_op jit(solution)/shard_map/while
  45.1 6.8 %copy-start = (bf16[5152,128]{1,0:T(8,128)(2,1)}, bf16[5152,128]{1,0:T(8,128)(2,1)S(1)}, u32[]{:S(2)}) copy-start(bf16[5152,128]{1,0:T(8,128)(2,1)S(1)} %reshape.49) | copy-start | bytes 3956740 | tf_op jit(solution)/shard_map/while
  56.0 4.6 %copy-start.4 = (bf16[640,512]{1,0:T(8,128)(2,1)S(1)}, bf16[640,512]{1,0:T(8,128)(2,1)}, u32[]{:S(2)}) copy-start(bf16[640,512]{1,0:T(8,128)(2,1)} %copy-done.3) | copy-start | bytes 1966084 | tf_op jit(solution)/shard_map/while
  60.7 4.8 %copy-start.3 = (bf16[640,512]{1,0:T(8,128)(2,1)}, bf16[640,512]{1,0:T(8,128)(2,1)S(1)}, u32[]{:S(2)}) copy-start(bf16[640,512]{1,0:T(8,128)(2,1)S(1)} %get-tuple-element.268) | copy-start | bytes 1966084 | tf_op jit(solution)/shard_map/while
  66.1 6.8 %copy-start = (bf16[5152,128]{1,0:T(8,128)(2,1)}, bf16[5152,128]{1,0:T(8,128)(2,1)S(1)}, u32[]{:S(2)}) copy-start(bf16[5152,128]{1,0:T(8,128)(2,1)S(1)} %reshape.49) | copy-start | bytes 3956740 | tf_op jit(solution)/shard_map/while
  77.1 4.6 %copy-start.4 = (bf16[640,512]{1,0:T(8,128)(2,1)S(1)}, bf16[640,512]{1,0:T(8,128)(2,1)}, u32[]{:S(2)}) copy-start(bf16[640,512]{1,0:T(8,128)(2,1)} %copy-done.3) | copy-start | bytes 1966084 | tf_op jit(solution)/shard_map/while
  81.8 4.8 %copy-start.3 = (bf16[640,512]{1,0:T(8,128)(2,1)}, bf16[640,512]{1,0:T(8,128)(2,1)S(1)}, u32[]{:S(2)}) copy-start(bf16[640,512]{1,0:T(8,128)(2,1)S(1)} %get-tuple-element.268) | copy-start | bytes 1966084 | tf_op jit(solution)/shard_map/while
  87.2 6.8 %copy-start = (bf16[5152,128]{1,0:T(8,128)(2,1)}, bf16[5152,128]{1,0:T(8,128)(2,1)S(1)}, u32[]{:S(2)}) copy-start(bf16[5152,128]{1,0:T(8,128)(2,1)S(1)} %reshape.49) | copy-start | bytes 3956740 | tf_op jit(solution)/shard_map/while
  98.2 4.6 %copy-start.4 = (bf16[640,512]{1,0:T(8,128)(2,1)S(1)}, bf16[640,512]{1,0:T(8,128)(2,1)}, u32[]{:S(2)}) copy-start(bf16[640,512]{1,0:T(8,128)(2,1)} %copy-done.3) | copy-start | bytes 1966084 | tf_op jit(solution)/shard_map/while
  102.8 4.8 %copy-start.3 = (bf16[640,512]{1,0:T(8,128)(2,1)}, bf16[640,512]{1,0:T(8,128)(2,1)S(1)}, u32[]{:S(2)}) copy-start(bf16[640,512]{1,0:T(8,128)(2,1)S(1)} %get-tuple-element.268) | copy-start | bytes 1966084 | tf_op jit(solution)/shard_map/while
  108.3 6.8 %copy-start = (bf16[5152,128]{1,0:T(8,128)(2,1)}, bf16[5152,128]{1,0:T(8,128)(2,1)S(1)}, u32[]{:S(2)}) copy-start(bf16[5152,128]{1,0:T(8,128)(2,1)S(1)} %reshape.49) | copy-start | bytes 3956740 | tf_op jit(solution)/shard_map/while
  119.3 4.6 %copy-start.4 = (bf16[640,512]{1,0:T(8,128)(2,1)S(1)}, bf16[640,512]{1,0:T(8,128)(2,1)}, u32[]{:S(2)}) copy-start(bf16[640,512]{1,0:T(8,128)(2,1)} %copy-done.3) | copy-start | bytes 1966084 | tf_op jit(solution)/shard_map/while
  123.9 4.8 %copy-start.3 = (bf16[640,512]{1,0:T(8,128)(2,1)}, bf16[640,512]{1,0:T(8,128)(2,1)S(1)}, u32[]{:S(2)}) copy-start(bf16[640,512]{1,0:T(8,128)(2,1)S(1)} %get-tuple-element.268) | copy-start | bytes 1966084 | tf_op jit(solution)/shard_map/while
  129.4 6.8 %copy-start = (bf16[5152,128]{1,0:T(8,128)(2,1)}, bf16[5152,128]{1,0:T(8,128)(2,1)S(1)}, u32[]{:S(2)}) copy-start(bf16[5152,128]{1,0:T(8,128)(2,1)S(1)} %reshape.49) | copy-start | bytes 3956740 | tf_op jit(solution)/shard_map/while
  145.0 4.8 %copy-start.3 = (bf16[640,512]{1,0:T(8,128)(2,1)}, bf16[640,512]{1,0:T(8,128)(2,1)S(1)}, u32[]{:S(2)}) copy-start(bf16[640,512]{1,0:T(8,128)(2,1)S(1)} %get-tuple-element.268) | copy-start | bytes 1966084 | tf_op jit(solution)/shard_map/while
  150.4 6.8 %copy-start = (bf16[5152,128]{1,0:T(8,128)(2,1)}, bf16[5152,128]{1,0:T(8,128)(2,1)S(1)}, u32[]{:S(2)}) copy-start(bf16[5152,128]{1,0:T(8,128)(2,1)S(1)} %reshape.49) | copy-start | bytes 3956740 | tf_op jit(solution)/shard_map/while
  166.1 4.8 %copy-start.3 = (bf16[640,512]{1,0:T(8,128)(2,1)}, bf16[640,512]{1,0:T(8,128)(2,1)S(1)}, u32[]{:S(2)}) copy-start(bf16[640,512]{1,0:T(8,128)(2,1)S(1)} %get-tuple-element.268) | copy-start | bytes 1966084 | tf_op jit(solution)/shard_map/while
  171.5 6.8 %copy-start = (bf16[5152,128]{1,0:T(8,128)(2,1)}, bf16[5152,128]{1,0:T(8,128)(2,1)S(1)}, u32[]{:S(2)}) copy-start(bf16[5152,128]{1,0:T(8,128)(2,1)S(1)} %reshape.49) | copy-start | bytes 3956740 | tf_op jit(solution)/shard_map/while
  182.5 4.6 %copy-start.4 = (bf16[640,512]{1,0:T(8,128)(2,1)S(1)}, bf16[640,512]{1,0:T(8,128)(2,1)}, u32[]{:S(2)}) copy-start(bf16[640,512]{1,0:T(8,128)(2,1)} %copy-done.3) | copy-start | bytes 1966084 | tf_op jit(solution)/shard_map/while
  187.1 4.8 %copy-start.3 = (bf16[640,512]{1,0:T(8,128)(2,1)}, bf16[640,512]{1,0:T(8,128)(2,1)S(1)}, u32[]{:S(2)}) copy-start(bf16[640,512]{1,0:T(8,128)(2,1)S(1)} %get-tuple-element.268) | copy-start | bytes 1966084 | tf_op jit(solution)/shard_map/while
  192.6 6.8 %copy-start = (bf16[5152,128]{1,0:T(8,128)(2,1)}, bf16[5152,128]{1,0:T(8,128)(2,1)S(1)}, u32[]{:S(2)}) copy-start(bf16[5152,128]{1,0:T(8,128)(2,1)S(1)} %reshape.49) | copy-start | bytes 3956740 | tf_op jit(solution)/shard_map/while
  (27 other events, 112.3 us)
Sparse Core Ops, SparseCore 0:
  214.0 33.2 reduce-scatter.1
where the time goes:
time: 256 us; the launch traced here: 254 us
  matrix products  72.2 us (28%)
  other arithmetic  41.2 us (16%)
  local copies, waits for them, and re-layouts  39 us (15%)
  waiting for transfers between devices  34.2 us (13%)
  loops' own time  27.2 us (11%)
  starting transfers between devices  26.7 us (10%)
  between operations  13.6 us (5%)
    dot_general x8, matrix products, window_attend(): jnp.einsum('wij,jd->wid', weights, outer_values, preferred_element_type=j...  35.7 us
    reduce_scatter x1, waiting for transfers between devices, local(): lax.psum_scatter(lax.dot_general(out_weight, attended, (((0,), (1,)), (()...  33.4 us
    reduce_sum x8, other arithmetic, window_attend(): row_total = jnp.sum(expon, axis=(0, 2), keepdims=True)  33 us
    dot_general x8, matrix products, window_attend(): jnp.einsum('wid,jd->wij', blended, outer_keys, preferred_element_type=jnp...  30.8 us
    another operation x1, loops' own time, local(): heads_out = lax.map(per_head, jnp.arange(head_count, dtype=jnp.int32))  27.2 us
    ppermute x10, starting transfers between devices, from_behind(): return lax.ppermute(shard, axis, pairs)  26.7 us
    reshape x16, local copies, waits for them, and re-layouts, lag_windows(): jnp.broadcast_to(padded[None], (span, length, feature_count))  14.1 us
    slice x24, local copies, waits for them, and re-layouts, lag_windows(): tiled[:span * (length - 1)].reshape(span, length - 1, feature_count)  11.2 us
  transfers between devices with their start and end apart: 11, of which 3 were waited for; matrix products, arithmetic and copies ran while one was open for 1% of the time, Pallas kernels for 0%

commit v1 on v0

v1 whole, which is shorter than its diff:
```python
import functools
import math

import jax
import jax.numpy as jnp
from jax import lax
from jax.experimental import pallas as pl
from jax.experimental.pallas import tpu as pltpu
from jax.sharding import PartitionSpec as P

HEAD_SIZE = 128
W1 = 512
W2 = 32
LAGS_PER_STEP = 2


def from_behind(shard, axis, by):
    length = lax.axis_size(axis)
    pairs = [(i, i + by) for i in range(length) if 0 <= i + by < length]
    return lax.ppermute(shard, axis, pairs)


def attend_kernel(
    query_ref, key_ref, value_ref, inner_key_ref, inner_value_ref, out_ref,
    keys, values, inner_keys, inner_values, inner_counts, scores,
):
    rows = query_ref.shape[0]
    heads = query_ref.shape[1] // HEAD_SIZE
    prior = key_ref.shape[0] // rows - 1
    middle = (prior - 1) * rows
    width = prior * rows
    span = inner_key_ref.shape[0] - rows
    steps = span // LAGS_PER_STEP
    step_rows = LAGS_PER_STEP * rows
    factor = HEAD_SIZE ** (-0.5) * math.log2(math.e)
    shard = lax.axis_index("seq")
    missing = jnp.maximum(prior - shard, 0)

    first_key = key_ref[pl.ds(pl.multiple_of(missing * rows, rows), 16), :][:1]
    for block in range(prior + 1):
        here = slice(block * rows, (block + 1) * rows)
        present = (block >= missing) if block < prior else None
        key_block, value_block = key_ref[here, :], value_ref[here, :]
        count = jnp.ones((rows, HEAD_SIZE), jnp.bfloat16)
        if present is not None:
            key_block = jnp.where(present, key_block, jnp.broadcast_to(first_key, key_block.shape))
            value_block = jnp.where(present, value_block, jnp.zeros_like(value_block))
            count = jnp.where(present, count, jnp.zeros_like(count))
        to = {0: 0, prior: 1}.get(block, block + 1)
        there = slice(to * rows, (to + 1) * rows)
        keys[there, :] = key_block
        values[there, :HEAD_SIZE] = value_block
        values[there, HEAD_SIZE:] = count

    inner_keys[...] = inner_key_ref[...].astype(jnp.float32)
    inner_values[...] = inner_value_ref[...].astype(jnp.float32)
    inner_counts[...] = jnp.ones((span + rows, HEAD_SIZE), jnp.float32)

    @pl.when(shard == 0)
    def _():
        inner_keys[:span, :] = jnp.broadcast_to(inner_keys[span : span + 1, :], (span, HEAD_SIZE))
        inner_values[:span, :] = jnp.zeros((span, HEAD_SIZE), jnp.float32)
        inner_counts[:span, :] = jnp.zeros((span, HEAD_SIZE), jnp.float32)

    row_index = lax.broadcasted_iota(jnp.int32, (rows, rows), 0)
    col_index = lax.broadcasted_iota(jnp.int32, (rows, rows), 1)
    oldest = col_index > row_index
    contract_last = (((1,), (1,)), ((), ()))

    def score_step(step, tops):
        blended = []
        for head in range(heads):
            query = query_ref[:, head * HEAD_SIZE : (head + 1) * HEAD_SIZE].astype(jnp.float32)
            for i in range(LAGS_PER_STEP):
                lag = step * LAGS_PER_STEP + i
                window = inner_keys[pl.ds(span - lag, rows), :]
                blended.append((query * window).astype(jnp.bfloat16))
        blended = jnp.concatenate(blended, axis=0)
        edge = lax.dot_general(
            blended, keys[: 2 * rows, :], contract_last, preferred_element_type=jnp.float32
        )
        rest = lax.dot_general(
            blended, keys[2 * rows :, :], contract_last, preferred_element_type=jnp.float32
        )
        result = []
        for head in range(heads):
            top = tops[head]
            for i in range(LAGS_PER_STEP):
                at = slice((head * LAGS_PER_STEP + i) * rows, (head * LAGS_PER_STEP + i + 1) * rows)
                both = jnp.where(oldest, edge[at, :rows], edge[at, rows:])
                to = pl.ds(pl.multiple_of((step * LAGS_PER_STEP + i) * rows, rows), rows)
                scores[head, to, :rows] = both
                scores[head, to, rows:] = rest[at, :]
                top = jnp.maximum(top, both)
                for block in range(prior - 1):
                    top = jnp.maximum(top, rest[at, block * rows : (block + 1) * rows])
            result.append(top)
        return tuple(result)

    lowest = jnp.full((rows, rows), -jnp.inf, jnp.float32)
    tops = lax.fori_loop(0, steps, score_step, (lowest,) * heads)
    tops = [
        jnp.broadcast_to(jnp.max(top, axis=1, keepdims=True), (rows, HEAD_SIZE)) for top in tops
    ]

    def value_step(step, totals):
        weights = []
        for head in range(heads):
            for i in range(LAGS_PER_STEP):
                at = pl.ds(pl.multiple_of((step * LAGS_PER_STEP + i) * rows, rows), rows)
                parts = []
                for block in range(prior):
                    part = scores[head, at, block * rows : (block + 1) * rows]
                    parts.append(jnp.exp2((part - tops[head]) * factor))
                edge = parts[0]
                parts = [jnp.where(oldest, edge, 0.0), jnp.where(oldest, 0.0, edge)] + parts[1:]
                weights.append(jnp.concatenate([part.astype(jnp.bfloat16) for part in parts], axis=1))
        weights = jnp.concatenate(weights, axis=0)
        summed = jnp.dot(weights, values[...], preferred_element_type=jnp.float32)
        result = []
        for head in range(heads):
            total, count = totals[head]
            for i in range(LAGS_PER_STEP):
                window = pl.ds(span - step * LAGS_PER_STEP - i, rows)
                at = slice((head * LAGS_PER_STEP + i) * rows, (head * LAGS_PER_STEP + i + 1) * rows)
                total = total + inner_values[window, :] * summed[at, :HEAD_SIZE]
                count = count + inner_counts[window, :] * summed[at, HEAD_SIZE:]
            result.append((total, count))
        return tuple(result)

    nothing = jnp.zeros((rows, HEAD_SIZE), jnp.float32)
    totals = lax.fori_loop(0, steps, value_step, ((nothing, nothing),) * heads)
    for head in range(heads):
        total, count = totals[head]
        out_ref[:, head * HEAD_SIZE : (head + 1) * HEAD_SIZE] = (total / count).astype(out_ref.dtype)


def attend(queries, keys, values, inner_keys, inner_values):
    rows = queries.shape[0]
    groups = keys.shape[1] // HEAD_SIZE
    heads = queries.shape[1] // keys.shape[1]
    outer = keys.shape[0]
    inner = inner_keys.shape[0]
    span = inner - rows
    width = outer - rows
    column = lambda g: (0, g)
    pairs = heads * groups * span * rows
    return pl.pallas_call(
        attend_kernel,
        grid=(groups,),
        out_shape=jax.ShapeDtypeStruct(queries.shape, queries.dtype),
        in_specs=[
            pl.BlockSpec((rows, heads * HEAD_SIZE), column),
            pl.BlockSpec((outer, HEAD_SIZE), column),
            pl.BlockSpec((outer, HEAD_SIZE), column),
            pl.BlockSpec((inner, HEAD_SIZE), column),
            pl.BlockSpec((inner, HEAD_SIZE), column),
        ],
        out_specs=pl.BlockSpec((rows, heads * HEAD_SIZE), column),
        scratch_shapes=[
            pltpu.VMEM((outer, HEAD_SIZE), jnp.bfloat16),
            pltpu.VMEM((outer, 2 * HEAD_SIZE), jnp.bfloat16),
            pltpu.VMEM((inner, HEAD_SIZE), jnp.float32),
            pltpu.VMEM((inner, HEAD_SIZE), jnp.float32),
            pltpu.VMEM((inner, HEAD_SIZE), jnp.float32),
            pltpu.VMEM((heads, span * rows, width), jnp.float32),
        ],
        compiler_params=pltpu.CompilerParams(vmem_limit_bytes=48 * 1024 * 1024),
        cost_estimate=pl.CostEstimate(
            flops=4 * pairs * outer * HEAD_SIZE,
            bytes_accessed=4 * queries.size + 4 * keys.size,
            transcendentals=pairs * width,
        ),
    )(queries, keys, values, inner_keys, inner_values)


def local(
    queries, first_key_rows, first_value_rows, second_key_rows, second_value_rows, out_weight
):
    row_count = queries.shape[0]
    shard_count = W1 // row_count
    prior_inner = from_behind(
        (second_key_rows[row_count - W2 :], second_value_rows[row_count - W2 :]), "seq", 1
    )
    pieces_keys = []
    pieces_values = []
    for distance in range(shard_count, 0, -1):
        arrived = from_behind((first_key_rows, first_value_rows), "seq", distance)
        pieces_keys.append(arrived[0])
        pieces_values.append(arrived[1])
    keys = jnp.concatenate(pieces_keys + [first_key_rows], axis=0)
    values = jnp.concatenate(pieces_values + [first_value_rows], axis=0)
    inner_keys = jnp.concatenate([prior_inner[0], second_key_rows], axis=0)
    inner_values = jnp.concatenate([prior_inner[1], second_value_rows], axis=0)
    attended = attend(queries, keys, values, inner_keys, inner_values)
    partial = jnp.dot(attended, out_weight, preferred_element_type=jnp.float32).astype(jnp.bfloat16)
    return lax.psum_scatter(partial, "head", scatter_dimension=1, tiled=True)


def solution(mesh):
    in_specs = (P("seq", "head"),) * 5 + (P("head", None),)
    return jax.shard_map(
        local, mesh=mesh, in_specs=in_specs, out_specs=P("seq", "head"), check_vma=False
    )
```

time: 256 us -> 129 us (0.50)
  matrix products: 72.2 us -> 2.24 us
  Pallas kernels: 0 us -> 50 us
  other arithmetic: 41.2 us -> 1.84 us
  local copies, waits for them, and re-layouts: 39 us -> 4.39 us
  loops' own time: 27.2 us -> 0 us
    dot_general x17 -> x1, matrix products: 72.2 us -> 2.24 us  [local(): jnp.dot(attended, out_weight, preferred_element_type=jnp.float32)]
    pallas_call x0 -> x1, Pallas kernels: none -> 50 us  [attend(): pl.pallas_call(attend_kernel, grid=(groups,), out_shape=jax.ShapeDtypeStr...]
    reduce_sum x8 -> x0, other arithmetic: 33 us -> none  [window_attend(): row_total = jnp.sum(expon, axis=(0, 2), keepdims=True)]
    another operation x1 -> x0, loops' own time: 27.2 us -> none  [local(): heads_out = lax.map(per_head, jnp.arange(head_count, dtype=jnp.int32))]
    reshape x16 -> x0, local copies, waits for them, and re-layouts: 14.1 us -> none  [lag_windows(): jnp.broadcast_to(padded[None], (span, length, feature_count))]
    slice x24 -> x0, local copies, waits for them, and re-layouts: 11.2 us -> none  [lag_windows(): tiled[:span * (length - 1)].reshape(span, length - 1, feature_count)]
    convert_element_type x8 -> x0, other arithmetic: 6.19 us -> none  [window_attend(): query_block.astype(jnp.float32)[None] * inner_key_win.astype(jnp.float32)]
    dynamic_slice x16 -> x0, local copies, waits for them, and re-layouts: 6.06 us -> none  [the longest x8 5.97 us: local(): heads_out = lax.map(per_head, jnp.arange(head_count, dtype=jnp.int32))]
  transfers between devices with their start and end apart: 11 -> 11, of which waited for: 3 -> 2; matrix products, arithmetic and copies ran while one was open for 1% -> 3% of each run, Pallas kernels for 0% -> 0%
where the time goes in v1:
time: 129 us
  Pallas kernels  50 us (39%)
  waiting for transfers between devices  31.9 us (25%)
  starting transfers between devices  24.8 us (19%)
  between operations  13.6 us (11%)
  local copies, waits for them, and re-layouts  4.39 us (3%)
  matrix products  2.24 us (2%)
  other arithmetic  1.84 us (1%)
    pallas_call x1, Pallas kernels, attend(): pl.pallas_call(attend_kernel, grid=(groups,), out_shape=jax.ShapeDtypeStr...  50 us
    reduce_scatter x1, waiting for transfers between devices, local(): return lax.psum_scatter(partial, 'head', scatter_dimension=1, tiled=True)  30.7 us
    ppermute x10, starting transfers between devices, from_behind(): return lax.ppermute(shard, axis, pairs)  24.8 us
  transfers between devices with their start and end apart: 11, of which 2 were waited for; matrix products, arithmetic and copies ran while one was open for 3% of the time, Pallas kernels for 0%

profile of v1, /device:TPU:0, one launch (start us, length us, event | category | flops | bytes accessed | tf_op | source)
XLA Modules:
  0.0 128.8 jit_solution(13715467173050964403)
XLA Ops:
  6.5 0.8 slice.6
  7.3 2.3 %collective-permute-start.8 = (bf16[32,512]{1,0:T(8,128)(2,1)S(1)}, bf16[32,512]{1,0:T(8,128)(2,1)S(1)}, u32[]{:S(2)}, u32[]{:S(2)}) collective-permute-start(bf16[32,512]{1,0:T(8,128)(2,1)S(1)} %slice.6), channel_id=1, source_target_pairs={{0,4},{4,8},{8,12},{12,16},{16,20},{20,24},{24,28},{1,5},{5,9},{9,... | collective-permute-start | bytes 98312 | tf_op jit(solution)/shard_map/ppermute | solution.py:20
  9.7 4.4 %collective-permute-start = (bf16[128,512]{1,0:T(8,128)(2,1)}, bf16[128,512]{1,0:T(8,128)(2,1)S(1)}, u32[]{:S(2)}, u32[]{:S(2)}) collective-permute-start(bf16[128,512]{1,0:T(8,128)(2,1)} %param.7), channel_id=1, source_target_pairs={{0,16},{4,20},{8,24},{12,28},{1,17},{5,21},{9,25},{13,29},{2,18},{... | collective-permute-start | bytes 393224 | tf_op jit(solution)/shard_map/ppermute | solution.py:20
  14.1 2.5 %collective-permute-start.1 = (bf16[128,512]{1,0:T(8,128)(2,1)}, bf16[128,512]{1,0:T(8,128)(2,1)S(1)}, u32[]{:S(2)}, u32[]{:S(2)}) collective-permute-start(bf16[128,512]{1,0:T(8,128)(2,1)} %param.7), channel_id=1, source_target_pairs={{0,12},{4,16},{8,20},{12,24},{16,28},{1,13},{5,17},{9,21},{13,25},... | collective-permute-start | bytes 393224 | tf_op jit(solution)/shard_map/ppermute | solution.py:20
  16.6 3.4 %collective-permute-start.2 = (bf16[128,512]{1,0:T(8,128)(2,1)}, bf16[128,512]{1,0:T(8,128)(2,1)S(1)}, u32[]{:S(2)}, u32[]{:S(2)}) collective-permute-start(bf16[128,512]{1,0:T(8,128)(2,1)} %param.7), channel_id=1, source_target_pairs={{0,8},{4,12},{8,16},{12,20},{16,24},{20,28},{1,9},{5,13},{9,17},{1... | collective-permute-start | bytes 393224 | tf_op jit(solution)/shard_map/ppermute | solution.py:20
  20.0 1.3 %collective-permute-start.3 = (bf16[128,512]{1,0:T(8,128)(2,1)}, bf16[128,512]{1,0:T(8,128)(2,1)S(1)}, u32[]{:S(2)}, u32[]{:S(2)}) collective-permute-start(bf16[128,512]{1,0:T(8,128)(2,1)} %param.7), channel_id=1, source_target_pairs={{0,4},{4,8},{8,12},{12,16},{16,20},{20,24},{24,28},{1,5},{5,9},{9,... | collective-permute-start | bytes 393224 | tf_op jit(solution)/shard_map/ppermute | solution.py:20
  21.3 0.8 slice.7
  22.1 0.0 collective-permute-done.8
  22.1 2.6 %collective-permute-start.9 = (bf16[32,512]{1,0:T(8,128)(2,1)S(1)}, bf16[32,512]{1,0:T(8,128)(2,1)S(1)}, u32[]{:S(2)}, u32[]{:S(2)}) collective-permute-start(bf16[32,512]{1,0:T(8,128)(2,1)S(1)} %slice.7), channel_id=1, source_target_pairs={{0,4},{4,8},{8,12},{12,16},{16,20},{20,24},{24,28},{1,5},{5,9},{9,... | collective-permute-start | bytes 98312 | tf_op jit(solution)/shard_map/ppermute | solution.py:20
  24.7 0.9 pad_maximum_fusion.inner_key_ref
  25.6 0.0 collective-permute-done.9
  25.6 3.6 %collective-permute-start.4 = (bf16[128,512]{1,0:T(8,128)(2,1)}, bf16[128,512]{1,0:T(8,128)(2,1)S(1)}, u32[]{:S(2)}, u32[]{:S(2)}) collective-permute-start(bf16[128,512]{1,0:T(8,128)(2,1)} %param.8), channel_id=1, source_target_pairs={{0,16},{4,20},{8,24},{12,28},{1,17},{5,21},{9,25},{13,29},{2,18},{... | collective-permute-start | bytes 393224 | tf_op jit(solution)/shard_map/ppermute | solution.py:20
  29.2 0.9 pad_maximum_fusion.1.inner_value_ref
  30.2 0.0 collective-permute-done
  30.2 1.3 %collective-permute-start.5 = (bf16[128,512]{1,0:T(8,128)(2,1)}, bf16[128,512]{1,0:T(8,128)(2,1)S(1)}, u32[]{:S(2)}, u32[]{:S(2)}) collective-permute-start(bf16[128,512]{1,0:T(8,128)(2,1)} %param.8), channel_id=1, source_target_pairs={{0,12},{4,16},{8,20},{12,24},{16,28},{1,13},{5,17},{9,21},{13,25},... | collective-permute-start | bytes 393224 | tf_op jit(solution)/shard_map/ppermute | solution.py:20
  31.5 0.0 collective-permute-done.1
  31.5 1.9 %collective-permute-start.6 = (bf16[128,512]{1,0:T(8,128)(2,1)}, bf16[128,512]{1,0:T(8,128)(2,1)S(1)}, u32[]{:S(2)}, u32[]{:S(2)}) collective-permute-start(bf16[128,512]{1,0:T(8,128)(2,1)} %param.8), channel_id=1, source_target_pairs={{0,8},{4,12},{8,16},{12,20},{16,24},{20,28},{1,9},{5,13},{9,17},{1... | collective-permute-start | bytes 393224 | tf_op jit(solution)/shard_map/ppermute | solution.py:20
  33.4 0.0 collective-permute-done.2
  33.4 1.4 %collective-permute-start.7 = (bf16[128,512]{1,0:T(8,128)(2,1)}, bf16[128,512]{1,0:T(8,128)(2,1)S(1)}, u32[]{:S(2)}, u32[]{:S(2)}) collective-permute-start(bf16[128,512]{1,0:T(8,128)(2,1)} %param.8), channel_id=1, source_target_pairs={{0,4},{4,8},{8,12},{12,16},{16,20},{20,24},{24,28},{1,5},{5,9},{9,... | collective-permute-start | bytes 393224 | tf_op jit(solution)/shard_map/ppermute | solution.py:20
  34.9 0.0 collective-permute-done.3
  34.9 0.9 constant_dynamic-update-slice_fusion.key_ref
  35.8 0.0 collective-permute-done.4
  35.9 0.0 collective-permute-done.5
  35.9 1.2 collective-permute-done.6
  37.1 0.0 collective-permute-done.7
  37.1 0.9 constant_dynamic-update-slice_fusion.5.value_ref
  38.0 0.0 copy-start
  38.0 0.9 copy-done
  39.0 50.0 %shard_map.64 = bf16[128,1024]{1,0:T(8,128)(2,1)S(1)} custom-call(bf16[128,1024]{1,0:T(8,128)(2,1)S(1)} %copy-done, bf16[640,512]{1,0:T(8,128)(2,1)S(1)} %constant_dynamic-update-slice_fusion.key_ref, bf16[640,512]{1,0:T(8,128)(2,1)S(1)} %constant_dynamic-update-slice_fusion.5.value_ref, bf16[160,512]{1,0:T(8,128)(2,1)S(1)} %pad_maximum_fusion.inner_key_ref, ...), custom_call_target="tpu_custom_call" | custom-call | flops 10737418240 | bytes 1835008 | tf_op jit(solution)/shard_map/pallas_call | solution.py:148
  89.0 2.2 %convolution_convert_fusion = bf16[128,4096]{1,0:T(8,128)(2,1)} fusion(bf16[128,1024]{1,0:T(8,128)(2,1)S(1)} %shard_map.64, bf16[1024,4096]{1,0:T(8,128)(2,1)S(1)} %copy-done.1), kind=kOutput, calls=%fused_computation | convolution fusion | flops 1074266112 | bytes 9699328 | tf_op jit(solution)/shard_map/dot_general | solution.py:196
  91.2 0.0 reduce-scatter.2.cloned.1.call-update
  91.2 30.7 %reduce-scatter.2.cloned.1.call-done = bf16[128,1024]{1,0:T(8,128)(2,1)} async-done(((bf16[128,4096]{1,0:T(8,128)(2,1)}), bf16[128,1024]{1,0:T(8,128)(2,1)}) %reduce-scatter.2.cloned.1.call-update) | async-done | bytes 262160 | tf_op jit(solution)/shard_map/reduce_scatter | solution.py:197
  (11 shorter events, 0.1 us)
Async XLA Ops:
  6.5 115.4 %reduce-scatter.2.cloned.1.call-start = ((), (), s32[]{:S(2)}) async-start(), calls=%async_computation.1 | async-start | bytes 1310720 | tf_op jit(solution)/shard_map/reduce_scatter | solution.py:197
  7.3 14.8 %collective-permute-start.8 = (bf16[32,512]{1,0:T(8,128)(2,1)S(1)}, bf16[32,512]{1,0:T(8,128)(2,1)S(1)}, u32[]{:S(2)}, u32[]{:S(2)}) collective-permute-start(bf16[32,512]{1,0:T(8,128)(2,1)S(1)} %slice.6), channel_id=1, source_target_pairs={{0,4},{4,8},{8,12},{12,16},{16,20},{20,24},{24,28},{1,5},{5,9},{9,... | collective-permute-start | bytes 98312 | tf_op jit(solution)/shard_map/ppermute | solution.py:20
  9.7 20.5 %collective-permute-start = (bf16[128,512]{1,0:T(8,128)(2,1)}, bf16[128,512]{1,0:T(8,128)(2,1)S(1)}, u32[]{:S(2)}, u32[]{:S(2)}) collective-permute-start(bf16[128,512]{1,0:T(8,128)(2,1)} %param.7), channel_id=1, source_target_pairs={{0,16},{4,20},{8,24},{12,28},{1,17},{5,21},{9,25},{13,29},{2,18},{... | collective-permute-start | bytes 393224 | tf_op jit(solution)/shard_map/ppermute | solution.py:20
  14.1 17.4 %collective-permute-start.1 = (bf16[128,512]{1,0:T(8,128)(2,1)}, bf16[128,512]{1,0:T(8,128)(2,1)S(1)}, u32[]{:S(2)}, u32[]{:S(2)}) collective-permute-start(bf16[128,512]{1,0:T(8,128)(2,1)} %param.7), channel_id=1, source_target_pairs={{0,12},{4,16},{8,20},{12,24},{16,28},{1,13},{5,17},{9,21},{13,25},... | collective-permute-start | bytes 393224 | tf_op jit(solution)/shard_map/ppermute | solution.py:20
  16.6 16.8 %collective-permute-start.2 = (bf16[128,512]{1,0:T(8,128)(2,1)}, bf16[128,512]{1,0:T(8,128)(2,1)S(1)}, u32[]{:S(2)}, u32[]{:S(2)}) collective-permute-start(bf16[128,512]{1,0:T(8,128)(2,1)} %param.7), channel_id=1, source_target_pairs={{0,8},{4,12},{8,16},{12,20},{16,24},{20,28},{1,9},{5,13},{9,17},{1... | collective-permute-start | bytes 393224 | tf_op jit(solution)/shard_map/ppermute | solution.py:20
  20.0 14.9 %collective-permute-start.3 = (bf16[128,512]{1,0:T(8,128)(2,1)}, bf16[128,512]{1,0:T(8,128)(2,1)S(1)}, u32[]{:S(2)}, u32[]{:S(2)}) collective-permute-start(bf16[128,512]{1,0:T(8,128)(2,1)} %param.7), channel_id=1, source_target_pairs={{0,4},{4,8},{8,12},{12,16},{16,20},{20,24},{24,28},{1,5},{5,9},{9,... | collective-permute-start | bytes 393224 | tf_op jit(solution)/shard_map/ppermute | solution.py:20
  22.1 3.6 %collective-permute-start.9 = (bf16[32,512]{1,0:T(8,128)(2,1)S(1)}, bf16[32,512]{1,0:T(8,128)(2,1)S(1)}, u32[]{:S(2)}, u32[]{:S(2)}) collective-permute-start(bf16[32,512]{1,0:T(8,128)(2,1)S(1)} %slice.7), channel_id=1, source_target_pairs={{0,4},{4,8},{8,12},{12,16},{16,20},{20,24},{24,28},{1,5},{5,9},{9,... | collective-permute-start | bytes 98312 | tf_op jit(solution)/shard_map/ppermute | solution.py:20
  25.6 10.2 %collective-permute-start.4 = (bf16[128,512]{1,0:T(8,128)(2,1)}, bf16[128,512]{1,0:T(8,128)(2,1)S(1)}, u32[]{:S(2)}, u32[]{:S(2)}) collective-permute-start(bf16[128,512]{1,0:T(8,128)(2,1)} %param.8), channel_id=1, source_target_pairs={{0,16},{4,20},{8,24},{12,28},{1,17},{5,21},{9,25},{13,29},{2,18},{... | collective-permute-start | bytes 393224 | tf_op jit(solution)/shard_map/ppermute | solution.py:20
  30.2 5.7 %collective-permute-start.5 = (bf16[128,512]{1,0:T(8,128)(2,1)}, bf16[128,512]{1,0:T(8,128)(2,1)S(1)}, u32[]{:S(2)}, u32[]{:S(2)}) collective-permute-start(bf16[128,512]{1,0:T(8,128)(2,1)} %param.8), channel_id=1, source_target_pairs={{0,12},{4,16},{8,20},{12,24},{16,28},{1,13},{5,17},{9,21},{13,25},... | collective-permute-start | bytes 393224 | tf_op jit(solution)/shard_map/ppermute | solution.py:20
  31.5 5.6 %collective-permute-start.6 = (bf16[128,512]{1,0:T(8,128)(2,1)}, bf16[128,512]{1,0:T(8,128)(2,1)S(1)}, u32[]{:S(2)}, u32[]{:S(2)}) collective-permute-start(bf16[128,512]{1,0:T(8,128)(2,1)} %param.8), channel_id=1, source_target_pairs={{0,8},{4,12},{8,16},{12,20},{16,24},{20,28},{1,9},{5,13},{9,17},{1... | collective-permute-start | bytes 393224 | tf_op jit(solution)/shard_map/ppermute | solution.py:20
  33.4 3.6 %collective-permute-start.7 = (bf16[128,512]{1,0:T(8,128)(2,1)}, bf16[128,512]{1,0:T(8,128)(2,1)S(1)}, u32[]{:S(2)}, u32[]{:S(2)}) collective-permute-start(bf16[128,512]{1,0:T(8,128)(2,1)} %param.8), channel_id=1, source_target_pairs={{0,4},{4,8},{8,12},{12,16},{16,20},{20,24},{24,28},{1,5},{5,9},{9,... | collective-permute-start | bytes 393224 | tf_op jit(solution)/shard_map/ppermute | solution.py:20
  38.0 1.0 copy-start
  39.0 50.0 %copy-start.1 = (bf16[1024,4096]{1,0:T(8,128)(2,1)S(1)}, bf16[1024,4096]{1,0:T(8,128)(2,1)}, u32[]{:S(2)}) copy-start(bf16[1024,4096]{1,0:T(8,128)(2,1)} %param.11) | copy-start | bytes 25165828
Sparse Core Ops, SparseCore 0:
  91.4 30.5 reduce-scatter.1

commit v2 on v1

v2 whole, which is shorter than its diff:
```python
import functools
import math

import jax
import jax.numpy as jnp
from jax import lax
from jax.experimental import pallas as pl
from jax.experimental.pallas import tpu as pltpu
from jax.sharding import PartitionSpec as P

HEAD_SIZE = 128
W1 = 512
W2 = 32
CHUNK_ROWS = 64
LAGS_PER_STEP = 4
MESH = pl.DeviceIdType.MESH


def layer_kernel(
    shards, owners,
    query_ref, key_ref, value_ref, inner_key_ref, inner_value_ref, weight_hbm, out_ref,
    outer, tail_keys, tail_values, inner_keys, inner_values, inner_counts,
    scores, attended, weight, partial, landed,
    outer_send, outer_recv, tail_send, tail_recv, part_send, part_recv, weight_sem,
):
    rows = query_ref.shape[0]
    groups = key_ref.shape[1] // HEAD_SIZE
    heads = query_ref.shape[1] // key_ref.shape[1]
    prior = outer.shape[1] // rows - 1
    span = tail_keys.shape[0]
    chunks = rows // CHUNK_ROWS
    steps = span // LAGS_PER_STEP
    own_width = out_ref.shape[1]
    factor = HEAD_SIZE ** (-0.5) * math.log2(math.e)
    shard = lax.axis_index("seq")
    owner = lax.axis_index("head")

    weight_copy = pltpu.make_async_copy(weight_hbm, weight, weight_sem)
    weight_copy.start()

    barrier = pltpu.get_barrier_semaphore()
    for distance in range(1, prior + 1):
        for to in (shard + distance, shard + shards - distance):
            pl.semaphore_signal(
                barrier, inc=1, device_id={"seq": lax.rem(to, shards)}, device_id_type=MESH
            )
    for offset in range(1, owners):
        pl.semaphore_signal(
            barrier, inc=1, device_id={"head": lax.rem(owner + offset, owners)}, device_id_type=MESH
        )

    def slot_of(block):
        return {0: 0, prior: 1}.get(block, block + 1)

    def block_rows(block):
        return pl.ds(slot_of(block) * rows, rows)

    own = block_rows(prior)
    for group in range(groups):
        columns = slice(group * HEAD_SIZE, (group + 1) * HEAD_SIZE)
        outer[group, own, :HEAD_SIZE] = key_ref[:, columns]
        outer[group, own, HEAD_SIZE : 2 * HEAD_SIZE] = value_ref[:, columns]
        outer[group, :, 2 * HEAD_SIZE :] = jnp.ones((outer.shape[1], HEAD_SIZE), jnp.bfloat16)

    pl.semaphore_wait(barrier, 2 * prior + owners - 1)

    def tail_copy(which):
        source, target = ((inner_key_ref, tail_keys), (inner_value_ref, tail_values))[which]
        return pltpu.make_async_remote_copy(
            src_ref=source.at[pl.ds(rows - span, span), :],
            dst_ref=target,
            send_sem=tail_send.at[which],
            recv_sem=tail_recv.at[which],
            device_id={"seq": lax.rem(shard + 1, shards)},
            device_id_type=MESH,
        )

    def outer_copy(group, distance):
        keys_values = pl.ds(0, 2 * HEAD_SIZE)
        return pltpu.make_async_remote_copy(
            src_ref=outer.at[group, own, keys_values],
            dst_ref=outer.at[group, block_rows(prior - distance), keys_values],
            send_sem=outer_send.at[group, distance - 1],
            recv_sem=outer_recv.at[group, distance - 1],
            device_id={"seq": lax.rem(shard + distance, shards)},
            device_id_type=MESH,
        )

    @pl.when(shard + 1 < shards)
    def _():
        tail_copy(0).start()
        tail_copy(1).start()

    for group in range(groups):
        for distance in range(prior, 0, -1):
            @pl.when(shard + distance < shards)
            def _():
                outer_copy(group, distance).start()

    for group in range(groups):
        columns = slice(group * HEAD_SIZE, (group + 1) * HEAD_SIZE)
        inner_keys[group, span:, :] = inner_key_ref[:, columns].astype(jnp.float32)
        inner_values[group, span:, :] = inner_value_ref[:, columns].astype(jnp.float32)
    inner_counts[...] = jnp.ones(inner_counts.shape, jnp.float32)

    @pl.when(shard == 0)
    def _():
        for group in range(groups):
            first = inner_keys[group, span : span + 1, :]
            inner_keys[group, :span, :] = jnp.broadcast_to(first, (span, HEAD_SIZE))
            inner_values[group, :span, :] = jnp.zeros((span, HEAD_SIZE), jnp.float32)
        inner_counts[:span, :] = jnp.zeros((span, HEAD_SIZE), jnp.float32)

    @pl.when(shard > 0)
    def _():
        tail_copy(0).wait_recv()
        tail_copy(1).wait_recv()
        for group in range(groups):
            columns = slice(group * HEAD_SIZE, (group + 1) * HEAD_SIZE)
            inner_keys[group, :span, :] = tail_keys[:, columns].astype(jnp.float32)
            inner_values[group, :span, :] = tail_values[:, columns].astype(jnp.float32)

    def receive(group):
        for distance in range(1, prior + 1):
            @pl.when(shard >= distance)
            def _():
                outer_copy(group, distance).wait_recv()

        for place in range(prior):
            @pl.when(shard == place)
            def _():
                first = outer[group, block_rows(prior - place), :HEAD_SIZE][:1]
                for block in range(prior - place):
                    outer[group, block_rows(block), :HEAD_SIZE] = jnp.broadcast_to(
                        first, (rows, HEAD_SIZE)
                    )
                    outer[group, block_rows(block), HEAD_SIZE:] = jnp.zeros(
                        (rows, 2 * HEAD_SIZE), jnp.bfloat16
                    )

    row_index = lax.broadcasted_iota(jnp.int32, (CHUNK_ROWS, rows), 0)
    col_index = lax.broadcasted_iota(jnp.int32, (CHUNK_ROWS, rows), 1)
    ahead = col_index - row_index
    contract_last = (((1,), (1,)), ((), ()))

    def place_of(item):
        group = lax.rem(item, groups)
        first_row = pl.multiple_of(lax.div(item, groups) * CHUNK_ROWS, CHUNK_ROWS)
        return group, first_row

    def part_rows(head, i):
        start = (head * LAGS_PER_STEP + i) * CHUNK_ROWS
        return slice(start, start + CHUNK_ROWS)

    def score_rows(step, i):
        return pl.ds(pl.multiple_of((step * LAGS_PER_STEP + i) * CHUNK_ROWS, CHUNK_ROWS), CHUNK_ROWS)

    def score_step(item, step, tops):
        group, first_row = place_of(item)
        oldest = ahead > first_row
        blended = []
        for head in range(heads):
            columns = pl.ds(
                pl.multiple_of((group * heads + head) * HEAD_SIZE, HEAD_SIZE), HEAD_SIZE
            )
            query = query_ref[pl.ds(first_row, CHUNK_ROWS), columns].astype(jnp.float32)
            for i in range(LAGS_PER_STEP):
                start = span + first_row - step * LAGS_PER_STEP - i
                window = inner_keys[group, pl.ds(start, CHUNK_ROWS), :]
                blended.append((query * window).astype(jnp.bfloat16))
        blended = jnp.concatenate(blended, axis=0)
        keys = outer[group, :, :HEAD_SIZE]
        edge = lax.dot_general(
            blended, keys[: 2 * rows], contract_last, preferred_element_type=jnp.float32
        )
        rest = lax.dot_general(
            blended, keys[2 * rows :], contract_last, preferred_element_type=jnp.float32
        )
        result = []
        for head in range(heads):
            top = tops[head]
            for i in range(LAGS_PER_STEP):
                at = part_rows(head, i)
                both = jnp.where(oldest, edge[at, :rows], edge[at, rows:])
                scores[head, score_rows(step, i), :rows] = both
                scores[head, score_rows(step, i), rows:] = rest[at, :]
                top = jnp.maximum(top, both)
                for block in range(prior - 1):
                    top = jnp.maximum(top, rest[at, block * rows : (block + 1) * rows])
            result.append(top)
        return tuple(result)

    def load_weights(item, step, tops):
        _, first_row = place_of(item)
        oldest = ahead > first_row
        weights = []
        for head in range(heads):
            for i in range(LAGS_PER_STEP):
                parts = []
                for block in range(prior):
                    part = scores[head, score_rows(step, i), block * rows : (block + 1) * rows]
                    parts.append(jnp.exp2((part - tops[head]) * factor))
                edge = parts[0]
                parts = [jnp.where(oldest, edge, 0.0), jnp.where(oldest, 0.0, edge)] + parts[1:]
                weights.append(jnp.concatenate([part.astype(jnp.bfloat16) for part in parts], axis=1))
        return jnp.concatenate(weights, axis=0)

    def value_step(item, step, tops, totals):
        group, first_row = place_of(item)
        weights = load_weights(item, step, tops)
        summed = jnp.dot(
            weights, outer[group, :, HEAD_SIZE:], preferred_element_type=jnp.float32
        )
        result = []
        for head in range(heads):
            total, count = totals[head]
            for i in range(LAGS_PER_STEP):
                window = pl.ds(span + first_row - step * LAGS_PER_STEP - i, CHUNK_ROWS)
                at = part_rows(head, i)
                total = total + inner_values[group, window, :] * summed[at, :HEAD_SIZE]
                count = count + inner_counts[window, :] * summed[at, HEAD_SIZE:]
            result.append((total, count))
        return tuple(result)

    lowest = (jnp.full((CHUNK_ROWS, rows), -jnp.inf, jnp.float32),) * heads
    zero = jnp.zeros((CHUNK_ROWS, HEAD_SIZE), jnp.float32)
    nothing = ((zero, zero),) * heads

    def finish_tops(tops):
        return tuple(
            jnp.broadcast_to(jnp.max(top, axis=1, keepdims=True), (CHUNK_ROWS, HEAD_SIZE))
            for top in tops
        )

    def part_copy(offset, first_row):
        chunk = lax.div(first_row, CHUNK_ROWS)
        at = pl.ds(first_row, CHUNK_ROWS)
        return pltpu.make_async_remote_copy(
            src_ref=partial.at[offset, at, :],
            dst_ref=landed.at[offset - 1, at, :],
            send_sem=part_send.at[offset - 1, chunk],
            recv_sem=part_recv.at[offset - 1, chunk],
            device_id={"head": lax.rem(owner + offset, owners)},
            device_id_type=MESH,
        )

    def finish_item(item, totals):
        group, first_row = place_of(item)
        for head in range(heads):
            total, count = totals[head]
            columns = pl.ds(
                pl.multiple_of((group * heads + head) * HEAD_SIZE, HEAD_SIZE), HEAD_SIZE
            )
            attended[:, columns] = (total / count).astype(jnp.bfloat16)

        @pl.when(group == groups - 1)
        def _():
            @pl.when(first_row == 0)
            def _():
                weight_copy.wait()

            for offset in list(range(1, owners)) + [0]:
                to = lax.rem(owner + offset, owners)
                columns = pl.ds(pl.multiple_of(to * own_width, own_width), own_width)
                partial[offset, pl.ds(first_row, CHUNK_ROWS), :] = jnp.dot(
                    attended[...], weight[:, columns], preferred_element_type=jnp.float32
                ).astype(jnp.bfloat16)
                if offset:
                    part_copy(offset, first_row).start()

    receive(0)
    tops = lax.fori_loop(0, steps, lambda step, tops: score_step(0, step, tops), lowest)

    def both_passes(item, tops):
        for group in range(1, groups):
            @pl.when(item == group)
            def _():
                receive(group)

        before = finish_tops(tops)

        def step_of(step, carry):
            now, totals = carry
            totals = value_step(item - 1, step, before, totals)
            return score_step(item, step, now), totals

        tops, totals = lax.fori_loop(0, steps, step_of, (lowest, nothing))
        finish_item(item - 1, totals)
        return tops

    items = groups * chunks
    tops = lax.fori_loop(1, items, both_passes, tops)
    before = finish_tops(tops)
    totals = lax.fori_loop(
        0, steps, lambda step, totals: value_step(items - 1, step, before, totals), nothing
    )
    finish_item(items - 1, totals)

    for group in range(groups):
        for distance in range(1, prior + 1):
            @pl.when(shard + distance < shards)
            def _():
                outer_copy(group, distance).wait_send()

    @pl.when(shard + 1 < shards)
    def _():
        tail_copy(0).wait_send()
        tail_copy(1).wait_send()

    for chunk in range(chunks):
        first_row = chunk * CHUNK_ROWS
        at = pl.ds(first_row, CHUNK_ROWS)
        total = partial[0, at, :].astype(jnp.float32)
        for offset in range(1, owners):
            part_copy(offset, first_row).wait_recv()
            total = total + landed[offset - 1, at, :].astype(jnp.float32)
        out_ref[at, :] = total.astype(out_ref.dtype)
    for chunk in range(chunks):
        for offset in range(1, owners):
            part_copy(offset, chunk * CHUNK_ROWS).wait_send()


def local(shards, owners, queries, first_keys, first_values, inner_keys, inner_values, out_weight):
    rows = queries.shape[0]
    groups = first_keys.shape[1] // HEAD_SIZE
    heads = queries.shape[1] // first_keys.shape[1]
    prior = W1 // rows
    outer = W1 + rows
    inner = W2 + rows
    features = out_weight.shape[1]
    chunks = rows // CHUNK_ROWS
    pairs = heads * groups * W2 * rows
    vmem = pl.BlockSpec(memory_space=pltpu.VMEM)
    dma = pltpu.SemaphoreType.DMA
    return pl.pallas_call(
        functools.partial(layer_kernel, shards, owners),
        out_shape=jax.ShapeDtypeStruct((rows, features // owners), queries.dtype),
        in_specs=[vmem] * 5 + [pl.BlockSpec(memory_space=pl.ANY)],
        out_specs=vmem,
        scratch_shapes=[
            pltpu.VMEM((groups, outer, 3 * HEAD_SIZE), jnp.bfloat16),
            pltpu.VMEM((W2, groups * HEAD_SIZE), jnp.bfloat16),
            pltpu.VMEM((W2, groups * HEAD_SIZE), jnp.bfloat16),
            pltpu.VMEM((groups, inner, HEAD_SIZE), jnp.float32),
            pltpu.VMEM((groups, inner, HEAD_SIZE), jnp.float32),
            pltpu.VMEM((inner, HEAD_SIZE), jnp.float32),
            pltpu.VMEM((heads, W2 * CHUNK_ROWS, W1), jnp.float32),
            pltpu.VMEM((CHUNK_ROWS, queries.shape[1]), jnp.bfloat16),
            pltpu.VMEM(out_weight.shape, jnp.bfloat16),
            pltpu.VMEM((owners, rows, features // owners), jnp.bfloat16),
            pltpu.VMEM((owners - 1, rows, features // owners), jnp.bfloat16),
            dma((groups, prior)),
            dma((groups, prior)),
            dma((2,)),
            dma((2,)),
            dma((owners - 1, chunks)),
            dma((owners - 1, chunks)),
            dma(()),
        ],
        compiler_params=pltpu.CompilerParams(
            collective_id=0, has_side_effects=True, vmem_limit_bytes=48 * 1024 * 1024
        ),
        cost_estimate=pl.CostEstimate(
            flops=4 * pairs * outer * HEAD_SIZE + 2 * rows * out_weight.size,
            bytes_accessed=2 * out_weight.size,
            transcendentals=pairs * W1,
        ),
    )(queries, first_keys, first_values, inner_keys, inner_values, out_weight)


def solution(mesh):
    in_specs = (P("seq", "head"),) * 5 + (P("head", None),)
    return jax.shard_map(
        functools.partial(local, mesh.shape["seq"], mesh.shape["head"]),
        mesh=mesh, in_specs=in_specs, out_specs=P("seq", "head"), check_vma=False,
    )
```

time: 129 us -> 79.5 us (0.62)
  the two profiles are of different devices: /device:TPU:0 before, /device:TPU:12 now
where the time goes in v2:
time: 79.5 us; the launch traced here: 79.3 us
  Pallas kernels  74 us (93%)
  local copies, waits for them, and re-layouts  5.27 us (7%)
    pallas_call x1, Pallas kernels, local(): pl.pallas_call(functools.partial(layer_kernel, shards, owners), out_shape...  74 us
    unnamed x11, local copies, waits for them, and re-layouts  5.27 us

profile of v2, /device:TPU:12, one launch (start us, length us, event | category | flops | bytes accessed | tf_op | source)
XLA Modules:
  0.0 79.3 jit_solution(3819003462308864156)
XLA Ops:
  0.0 0.0 copy-start
  0.0 0.9 %copy-done = bf16[128,1024]{1,0:T(8,128)(2,1)S(1)} copy-done((bf16[128,1024]{1,0:T(8,128)(2,1)S(1)}, bf16[128,1024]{1,0:T(8,128)(2,1)}, u32[]{:S(2)}) %copy-start) | copy-done | bytes 262168
  1.0 0.0 copy-start.1
  1.0 0.9 %copy-done.1 = bf16[128,512]{1,0:T(8,128)(2,1)S(1)} copy-done((bf16[128,512]{1,0:T(8,128)(2,1)S(1)}, bf16[128,512]{1,0:T(8,128)(2,1)}, u32[]{:S(2)}) %copy-start.1) | copy-done | bytes 131096
  1.9 0.0 copy-start.2
  1.9 0.9 %copy-done.2 = bf16[128,512]{1,0:T(8,128)(2,1)S(1)} copy-done((bf16[128,512]{1,0:T(8,128)(2,1)S(1)}, bf16[128,512]{1,0:T(8,128)(2,1)}, u32[]{:S(2)}) %copy-start.2) | copy-done | bytes 131096
  2.8 0.0 copy-start.3
  2.8 0.9 %copy-done.3 = bf16[128,512]{1,0:T(8,128)(2,1)S(1)} copy-done((bf16[128,512]{1,0:T(8,128)(2,1)S(1)}, bf16[128,512]{1,0:T(8,128)(2,1)}, u32[]{:S(2)}) %copy-start.3) | copy-done | bytes 131096
  3.7 0.0 copy-start.4
  3.7 0.9 %copy-done.4 = bf16[128,512]{1,0:T(8,128)(2,1)S(1)} copy-done((bf16[128,512]{1,0:T(8,128)(2,1)S(1)}, bf16[128,512]{1,0:T(8,128)(2,1)}, u32[]{:S(2)}) %copy-start.4) | copy-done | bytes 131096
  4.6 74.0 %shard_map.64 = bf16[128,1024]{1,0:T(8,128)(2,1)S(1)} custom-call(bf16[128,1024]{1,0:T(8,128)(2,1)S(1)} %copy-done, bf16[128,512]{1,0:T(8,128)(2,1)S(1)} %copy-done.1, bf16[128,512]{1,0:T(8,128)(2,1)S(1)} %copy-done.2, bf16[128,512]{1,0:T(8,128)(2,1)S(1)} %copy-done.3, bf16[128,512]{1,0:T(8,128)(2,1)S(1)} %copy-done.4, bf16[1024,4096]{1,0:T(8,128)(2,1)} %weight_hbm.1), custom_call_target="tpu_custom_call" | custom-call | flops 11811160064 | bytes 8388608 | tf_op jit(solution)/shard_map/pallas_call | solution.py:335
  78.6 0.7 copy.8
Async XLA Ops:
  0.0 0.9 %copy-start = (bf16[128,1024]{1,0:T(8,128)(2,1)S(1)}, bf16[128,1024]{1,0:T(8,128)(2,1)}, u32[]{:S(2)}) copy-start(bf16[128,1024]{1,0:T(8,128)(2,1)} %query_ref.1) | copy-start | bytes 786436
  1.0 0.9 %copy-start.1 = (bf16[128,512]{1,0:T(8,128)(2,1)S(1)}, bf16[128,512]{1,0:T(8,128)(2,1)}, u32[]{:S(2)}) copy-start(bf16[128,512]{1,0:T(8,128)(2,1)} %key_ref.1) | copy-start | bytes 393220
  1.9 0.9 %copy-start.2 = (bf16[128,512]{1,0:T(8,128)(2,1)S(1)}, bf16[128,512]{1,0:T(8,128)(2,1)}, u32[]{:S(2)}) copy-start(bf16[128,512]{1,0:T(8,128)(2,1)} %value_ref.1) | copy-start | bytes 393220
  2.8 0.9 %copy-start.3 = (bf16[128,512]{1,0:T(8,128)(2,1)S(1)}, bf16[128,512]{1,0:T(8,128)(2,1)}, u32[]{:S(2)}) copy-start(bf16[128,512]{1,0:T(8,128)(2,1)} %inner_key_ref.1) | copy-start | bytes 393220
  3.7 0.9 %copy-start.4 = (bf16[128,512]{1,0:T(8,128)(2,1)S(1)}, bf16[128,512]{1,0:T(8,128)(2,1)}, u32[]{:S(2)}) copy-start(bf16[128,512]{1,0:T(8,128)(2,1)} %inner_value_ref.1) | copy-start | bytes 393220

commit v3 on v2

--- a/solution.py
+++ b/solution.py
@@ -18,14 +18,15 @@
 
 def layer_kernel(
     shards, owners,
-    query_ref, key_ref, value_ref, inner_key_ref, inner_value_ref, weight_hbm, out_ref,
-    outer, tail_keys, tail_values, inner_keys, inner_values, inner_counts,
+    query_hbm, key_hbm, value_hbm, inner_key_hbm, inner_value_hbm, weight_hbm, out_ref,
+    query_ref, inner_key_ref, inner_value_ref,
+    outer, flipped, tail_keys, tail_values, inner_keys, inner_values,
     scores, attended, weight, partial, landed,
-    outer_send, outer_recv, tail_send, tail_recv, part_send, part_recv, weight_sem,
+    outer_send, outer_recv, tail_send, tail_recv, part_send, part_recv, weight_sem, load_sem, own_sem,
 ):
     rows = query_ref.shape[0]
-    groups = key_ref.shape[1] // HEAD_SIZE
-    heads = query_ref.shape[1] // key_ref.shape[1]
+    groups = outer.shape[0]
+    heads = query_ref.shape[1] // (groups * HEAD_SIZE)
     prior = outer.shape[1] // rows - 1
     span = tail_keys.shape[0]
     chunks = rows // CHUNK_ROWS
@@ -34,9 +35,6 @@
     factor = HEAD_SIZE ** (-0.5) * math.log2(math.e)
     shard = lax.axis_index("seq")
     owner = lax.axis_index("head")
-
-    weight_copy = pltpu.make_async_copy(weight_hbm, weight, weight_sem)
-    weight_copy.start()
 
     barrier = pltpu.get_barrier_semaphore()
     for distance in range(1, prior + 1):
@@ -56,11 +54,33 @@
         return pl.ds(slot_of(block) * rows, rows)
 
     own = block_rows(prior)
+
+    def own_copy(group, which):
+        return pltpu.make_async_copy(
+            (key_hbm, value_hbm)[which].at[:, pl.ds(group * HEAD_SIZE, HEAD_SIZE)],
+            outer.at[group, own, pl.ds(which * HEAD_SIZE, HEAD_SIZE)],
+            own_sem.at[group, which],
+        )
+
+    loads = [
+        pltpu.make_async_copy(source, target, load_sem.at[i])
+        for i, (source, target) in enumerate((
+            (inner_key_hbm, inner_key_ref), (inner_value_hbm, inner_value_ref),
+            (query_hbm, query_ref),
+        ))
+    ]
+    for load in loads:
+        load.start()
     for group in range(groups):
-        columns = slice(group * HEAD_SIZE, (group + 1) * HEAD_SIZE)
-        outer[group, own, :HEAD_SIZE] = key_ref[:, columns]
-        outer[group, own, HEAD_SIZE : 2 * HEAD_SIZE] = value_ref[:, columns]
-        outer[group, :, 2 * HEAD_SIZE :] = jnp.ones((outer.shape[1], HEAD_SIZE), jnp.bfloat16)
+        for which in range(2):
+            own_copy(group, which).start()
+    weight_copy = pltpu.make_async_copy(weight_hbm, weight, weight_sem)
+    weight_copy.start()
+    for load in loads:
+        load.wait()
+    for group in range(groups):
+        for which in range(2):
+            own_copy(group, which).wait()
 
     pl.semaphore_wait(barrier, 2 * prior + owners - 1)
 
@@ -101,7 +121,6 @@
         columns = slice(group * HEAD_SIZE, (group + 1) * HEAD_SIZE)
         inner_keys[group, span:, :] = inner_key_ref[:, columns].astype(jnp.float32)
         inner_values[group, span:, :] = inner_value_ref[:, columns].astype(jnp.float32)
-    inner_counts[...] = jnp.ones(inner_counts.shape, jnp.float32)
 
     @pl.when(shard == 0)
     def _():
@@ -109,7 +128,6 @@
             first = inner_keys[group, span : span + 1, :]
             inner_keys[group, :span, :] = jnp.broadcast_to(first, (span, HEAD_SIZE))
             inner_values[group, :span, :] = jnp.zeros((span, HEAD_SIZE), jnp.float32)
-        inner_counts[:span, :] = jnp.zeros((span, HEAD_SIZE), jnp.float32)
 
     @pl.when(shard > 0)
     def _():
@@ -120,27 +138,38 @@
             inner_keys[group, :span, :] = tail_keys[:, columns].astype(jnp.float32)
             inner_values[group, :span, :] = tail_values[:, columns].astype(jnp.float32)
 
+    count_rows = flipped.shape[1] - HEAD_SIZE
+
+    def flip(group, block):
+        there = slice(slot_of(block) * rows, (slot_of(block) + 1) * rows)
+        value = outer[group, block_rows(block), HEAD_SIZE:].astype(jnp.float32)
+        flipped[group, :HEAD_SIZE, there] = value.T.astype(jnp.bfloat16)
+        flipped[group, HEAD_SIZE:, there] = jnp.ones((count_rows, rows), jnp.bfloat16)
+
     def receive(group):
+        flip(group, prior)
         for distance in range(1, prior + 1):
             @pl.when(shard >= distance)
             def _():
                 outer_copy(group, distance).wait_recv()
+                flip(group, prior - distance)
 
         for place in range(prior):
             @pl.when(shard == place)
             def _():
                 first = outer[group, block_rows(prior - place), :HEAD_SIZE][:1]
                 for block in range(prior - place):
+                    there = slice(slot_of(block) * rows, (slot_of(block) + 1) * rows)
                     outer[group, block_rows(block), :HEAD_SIZE] = jnp.broadcast_to(
                         first, (rows, HEAD_SIZE)
                     )
-                    outer[group, block_rows(block), HEAD_SIZE:] = jnp.zeros(
-                        (rows, 2 * HEAD_SIZE), jnp.bfloat16
-                    )
-
-    row_index = lax.broadcasted_iota(jnp.int32, (CHUNK_ROWS, rows), 0)
-    col_index = lax.broadcasted_iota(jnp.int32, (CHUNK_ROWS, rows), 1)
-    ahead = col_index - row_index
+                    flipped[group, :, there] = jnp.zeros((flipped.shape[1], rows), jnp.bfloat16)
+
+    lanes = LAGS_PER_STEP * CHUNK_ROWS
+    pair_index = lax.broadcasted_iota(jnp.int32, (rows, lanes), 1)
+    ahead = lax.broadcasted_iota(jnp.int32, (rows, lanes), 0) - lax.rem(pair_index, CHUNK_ROWS)
+    pair_index = lax.broadcasted_iota(jnp.int32, (8, lanes), 1)
+    behind = lax.rem(pair_index, CHUNK_ROWS) - lax.div(pair_index, CHUNK_ROWS)
     contract_last = (((1,), (1,)), ((), ()))
 
     def place_of(item):
@@ -148,89 +177,93 @@
         first_row = pl.multiple_of(lax.div(item, groups) * CHUNK_ROWS, CHUNK_ROWS)
         return group, first_row
 
-    def part_rows(head, i):
-        start = (head * LAGS_PER_STEP + i) * CHUNK_ROWS
-        return slice(start, start + CHUNK_ROWS)
-
-    def score_rows(step, i):
-        return pl.ds(pl.multiple_of((step * LAGS_PER_STEP + i) * CHUNK_ROWS, CHUNK_ROWS), CHUNK_ROWS)
+    def windows_of(array, group, first_row, step):
+        start = span + first_row - step * LAGS_PER_STEP
+        return [array[group, pl.ds(start - i, CHUNK_ROWS), :] for i in range(LAGS_PER_STEP)]
+
+    def head_columns(group, head):
+        return pl.ds(pl.multiple_of((group * heads + head) * HEAD_SIZE, HEAD_SIZE), HEAD_SIZE)
+
+    def by_eight(array):
+        return array.reshape(array.shape[0] // 8, 8, array.shape[1])
 
     def score_step(item, step, tops):
         group, first_row = place_of(item)
         oldest = ahead > first_row
-        blended = []
-        for head in range(heads):
-            columns = pl.ds(
-                pl.multiple_of((group * heads + head) * HEAD_SIZE, HEAD_SIZE), HEAD_SIZE
-            )
-            query = query_ref[pl.ds(first_row, CHUNK_ROWS), columns].astype(jnp.float32)
-            for i in range(LAGS_PER_STEP):
-                start = span + first_row - step * LAGS_PER_STEP - i
-                window = inner_keys[group, pl.ds(start, CHUNK_ROWS), :]
-                blended.append((query * window).astype(jnp.bfloat16))
-        blended = jnp.concatenate(blended, axis=0)
+        windows = windows_of(inner_keys, group, first_row, step)
         keys = outer[group, :, :HEAD_SIZE]
-        edge = lax.dot_general(
-            blended, keys[: 2 * rows], contract_last, preferred_element_type=jnp.float32
-        )
-        rest = lax.dot_general(
-            blended, keys[2 * rows :], contract_last, preferred_element_type=jnp.float32
-        )
         result = []
         for head in range(heads):
-            top = tops[head]
-            for i in range(LAGS_PER_STEP):
-                at = part_rows(head, i)
-                both = jnp.where(oldest, edge[at, :rows], edge[at, rows:])
-                scores[head, score_rows(step, i), :rows] = both
-                scores[head, score_rows(step, i), rows:] = rest[at, :]
-                top = jnp.maximum(top, both)
-                for block in range(prior - 1):
-                    top = jnp.maximum(top, rest[at, block * rows : (block + 1) * rows])
-            result.append(top)
+            query = query_ref[pl.ds(first_row, CHUNK_ROWS), head_columns(group, head)]
+            query = query.astype(jnp.float32)
+            blended = jnp.concatenate(
+                [(query * window).astype(jnp.bfloat16) for window in windows], axis=0
+            )
+            product = lax.dot_general(
+                keys, blended, contract_last, preferred_element_type=jnp.float32
+            )
+            both = jnp.where(oldest, product[:rows], product[rows : 2 * rows])
+            rest = product[2 * rows :]
+            scores[head, step, :rows, :] = both
+            scores[head, step, rows:, :] = rest
+            top = jnp.maximum(jnp.max(by_eight(both), axis=0), jnp.max(by_eight(rest), axis=0))
+            result.append(jnp.maximum(tops[head], top))
         return tuple(result)
-
-    def load_weights(item, step, tops):
-        _, first_row = place_of(item)
-        oldest = ahead > first_row
-        weights = []
-        for head in range(heads):
-            for i in range(LAGS_PER_STEP):
-                parts = []
-                for block in range(prior):
-                    part = scores[head, score_rows(step, i), block * rows : (block + 1) * rows]
-                    parts.append(jnp.exp2((part - tops[head]) * factor))
-                edge = parts[0]
-                parts = [jnp.where(oldest, edge, 0.0), jnp.where(oldest, 0.0, edge)] + parts[1:]
-                weights.append(jnp.concatenate([part.astype(jnp.bfloat16) for part in parts], axis=1))
-        return jnp.concatenate(weights, axis=0)
 
     def value_step(item, step, tops, totals):
         group, first_row = place_of(item)
-        weights = load_weights(item, step, tops)
-        summed = jnp.dot(
-            weights, outer[group, :, HEAD_SIZE:], preferred_element_type=jnp.float32
-        )
+        oldest = ahead > first_row
+        windows = jnp.concatenate(windows_of(inner_values, group, first_row, step), axis=0).T
+        counted = (behind + first_row >= step * LAGS_PER_STEP) | (shard > 0)
+        counted = jnp.where(counted, 1.0, 0.0)
         result = []
         for head in range(heads):
             total, count = totals[head]
-            for i in range(LAGS_PER_STEP):
-                window = pl.ds(span + first_row - step * LAGS_PER_STEP - i, CHUNK_ROWS)
-                at = part_rows(head, i)
-                total = total + inner_values[group, window, :] * summed[at, :HEAD_SIZE]
-                count = count + inner_counts[window, :] * summed[at, HEAD_SIZE:]
+            part = by_eight(scores[head, step])
+            part = jnp.exp2((part - tops[head][None]) * factor).reshape(prior * rows, lanes)
+            edge = part[:rows]
+            weights = jnp.concatenate(
+                [
+                    jnp.where(oldest, edge, 0.0).astype(jnp.bfloat16),
+                    jnp.where(oldest, 0.0, edge).astype(jnp.bfloat16),
+                    part[rows:].astype(jnp.bfloat16),
+                ],
+                axis=0,
+            )
+            summed = jnp.dot(flipped[group], weights, preferred_element_type=jnp.float32)
+            gain = windows * summed[:HEAD_SIZE]
+            pairs = counted * summed[HEAD_SIZE : HEAD_SIZE + 8]
+            for start in range(0, lanes, HEAD_SIZE):
+                total = total + gain[:, start : start + HEAD_SIZE]
+                count = count + pairs[:, start : start + HEAD_SIZE]
             result.append((total, count))
         return tuple(result)
 
-    lowest = (jnp.full((CHUNK_ROWS, rows), -jnp.inf, jnp.float32),) * heads
-    zero = jnp.zeros((CHUNK_ROWS, HEAD_SIZE), jnp.float32)
-    nothing = ((zero, zero),) * heads
+    lowest = (jnp.full((8, lanes), -jnp.inf, jnp.float32),) * heads
+    nothing = (
+        (
+            jnp.zeros((HEAD_SIZE, HEAD_SIZE), jnp.float32),
+            jnp.zeros((8, HEAD_SIZE), jnp.float32),
+        ),
+    ) * heads
+
+    def fold(array, combine):
+        shift = CHUNK_ROWS
+        while shift < HEAD_SIZE:
+            array = combine(array, pltpu.roll(array, shift, 1))
+            shift *= 2
+        return array
 
     def finish_tops(tops):
-        return tuple(
-            jnp.broadcast_to(jnp.max(top, axis=1, keepdims=True), (CHUNK_ROWS, HEAD_SIZE))
-            for top in tops
-        )
+        result = []
+        for top in tops:
+            most = top[:, :HEAD_SIZE]
+            for start in range(HEAD_SIZE, lanes, HEAD_SIZE):
+                most = jnp.maximum(most, top[:, start : start + HEAD_SIZE])
+            most = jnp.max(fold(most, jnp.maximum), axis=0, keepdims=True)
+            most = jnp.broadcast_to(most, (8, HEAD_SIZE))
+            result.append(jnp.concatenate([most] * (lanes // HEAD_SIZE), axis=1))
+        return tuple(result)
 
     def part_copy(offset, first_row):
         chunk = lax.div(first_row, CHUNK_ROWS)
@@ -247,11 +280,9 @@
     def finish_item(item, totals):
         group, first_row = place_of(item)
         for head in range(heads):
-            total, count = totals[head]
-            columns = pl.ds(
-                pl.multiple_of((group * heads + head) * HEAD_SIZE, HEAD_SIZE), HEAD_SIZE
-            )
-            attended[:, columns] = (total / count).astype(jnp.bfloat16)
+            total, count = (fold(array, jnp.add) for array in totals[head])
+            mean = (by_eight(total) / count[None]).reshape(total.shape).T
+            attended[:, head_columns(group, head)] = mean[:CHUNK_ROWS].astype(jnp.bfloat16)
 
         @pl.when(group == groups - 1)
         def _():
@@ -335,16 +366,21 @@
     return pl.pallas_call(
         functools.partial(layer_kernel, shards, owners),
         out_shape=jax.ShapeDtypeStruct((rows, features // owners), queries.dtype),
-        in_specs=[vmem] * 5 + [pl.BlockSpec(memory_space=pl.ANY)],
+        in_specs=[pl.BlockSpec(memory_space=pltpu.HBM)] * 6,
         out_specs=vmem,
         scratch_shapes=[
-            pltpu.VMEM((groups, outer, 3 * HEAD_SIZE), jnp.bfloat16),
+            pltpu.VMEM(queries.shape, jnp.bfloat16),
+            pltpu.VMEM(inner_keys.shape, jnp.bfloat16),
+            pltpu.VMEM(inner_keys.shape, jnp.bfloat16),
+            pltpu.VMEM((groups, outer, 2 * HEAD_SIZE), jnp.bfloat16),
+            pltpu.VMEM((groups, HEAD_SIZE + 16, outer), jnp.bfloat16),
             pltpu.VMEM((W2, groups * HEAD_SIZE), jnp.bfloat16),
             pltpu.VMEM((W2, groups * HEAD_SIZE), jnp.bfloat16),
             pltpu.VMEM((groups, inner, HEAD_SIZE), jnp.float32),
             pltpu.VMEM((groups, inner, HEAD_SIZE), jnp.float32),
-            pltpu.VMEM((inner, HEAD_SIZE), jnp.float32),
-            pltpu.VMEM((heads, W2 * CHUNK_ROWS, W1), jnp.float32),
+            pltpu.VMEM(
+                (heads, W2 // LAGS_PER_STEP, W1, LAGS_PER_STEP * CHUNK_ROWS), jnp.float32
+            ),
             pltpu.VMEM((CHUNK_ROWS, queries.shape[1]), jnp.bfloat16),
             pltpu.VMEM(out_weight.shape, jnp.bfloat16),
             pltpu.VMEM((owners, rows, features // owners), jnp.bfloat16),
@@ -356,9 +392,11 @@
             dma((owners - 1, chunks)),
             dma((owners - 1, chunks)),
             dma(()),
+            dma((3,)),
+            dma((groups, 2)),
         ],
         compiler_params=pltpu.CompilerParams(
-            collective_id=0, has_side_effects=True, vmem_limit_bytes=48 * 1024 * 1024
+            collective_id=0, has_side_effects=True, vmem_limit_bytes=64 * 1024 * 1024 - 2**17
         ),
         cost_estimate=pl.CostEstimate(
             flops=4 * pairs * outer * HEAD_SIZE + 2 * rows * out_weight.size,

time: 79.5 us -> 76 us (0.956)
  local copies, waits for them, and re-layouts: 5.27 us -> 1.67 us
    unnamed x11 -> x1, local copies, waits for them, and re-layouts: 5.27 us -> 1.67 us
where the time goes in v3:
time: 76 us; the launch traced here: 75.8 us
  Pallas kernels  74.1 us (97%)
  local copies, waits for them, and re-layouts  1.67 us (2%)
    pallas_call x1, Pallas kernels, local(): pl.pallas_call(functools.partial(layer_kernel, shards, owners), out_shape...  74.1 us
    unnamed x1, local copies, waits for them, and re-layouts  1.67 us

profile of v3, /device:TPU:12, one launch (start us, length us, event | category | flops | bytes accessed | tf_op | source)
XLA Modules:
  0.0 75.8 jit_solution(7019574547020754287)
XLA Ops:
  0.0 74.1 %shard_map.64 = bf16[128,1024]{1,0:T(8,128)(2,1)} custom-call(bf16[128,1024]{1,0:T(8,128)(2,1)} %query_hbm.1, bf16[128,512]{1,0:T(8,128)(2,1)} %key_hbm.1, bf16[128,512]{1,0:T(8,128)(2,1)} %value_hbm.1, bf16[128,512]{1,0:T(8,128)(2,1)} %inner_key_hbm.1, bf16[128,512]{1,0:T(8,128)(2,1)} %inner_value_hbm.1, bf16[1024,4096]{1,0:T(8,128)(2,1)} %weight_hbm.1), custom_call_target="tpu_custom_call" | custom-call | flops 11811160064 | bytes 8388608 | tf_op jit(solution)/shard_map/pallas_call | solution.py:366
  74.2 1.7 %copy.8 = bf16[128,1024]{1,0:T(8,128)(2,1)} copy(bf16[128,1024]{1,0:T(8,128)(2,1)} %shard_map.64) | data formatting | bytes 524288

commit v4 on v3

--- a/solution.py
+++ b/solution.py
@@ -23,6 +23,7 @@
     outer, flipped, tail_keys, tail_values, inner_keys, inner_values,
     scores, attended, weight, partial, landed,
     outer_send, outer_recv, tail_send, tail_recv, part_send, part_recv, weight_sem, load_sem, own_sem,
+    hand_send,
 ):
     rows = query_ref.shape[0]
     groups = outer.shape[0]
@@ -37,7 +38,8 @@
     owner = lax.axis_index("head")
 
     barrier = pltpu.get_barrier_semaphore()
-    for distance in range(1, prior + 1):
+    direct = range(2, prior + 1, 2)
+    for distance in (1, *direct):
         for to in (shard + distance, shard + shards - distance):
             pl.semaphore_signal(
                 barrier, inc=1, device_id={"seq": lax.rem(to, shards)}, device_id_type=MESH
@@ -82,7 +84,7 @@
         for which in range(2):
             own_copy(group, which).wait()
 
-    pl.semaphore_wait(barrier, 2 * prior + owners - 1)
+    pl.semaphore_wait(barrier, 2 * (1 + len(direct)) + owners - 1)
 
     def tail_copy(which):
         source, target = ((inner_key_ref, tail_keys), (inner_value_ref, tail_values))[which]
@@ -111,11 +113,48 @@
         tail_copy(0).start()
         tail_copy(1).start()
 
+    even = lax.rem(shard, 2) == 0
+
+    def hand_on(group, distance, to_distance, to):
+        keys_values = pl.ds(0, 2 * HEAD_SIZE)
+        return pltpu.make_async_remote_copy(
+            src_ref=outer.at[group, block_rows(prior - distance), keys_values],
+            dst_ref=outer.at[group, block_rows(prior - to_distance), keys_values],
+            send_sem=hand_send.at[group, distance // 2],
+            recv_sem=outer_recv.at[group, to_distance - 1],
+            device_id={"seq": to},
+            device_id_type=MESH,
+        )
+
+    def hand_up(group, distance):
+        return hand_on(group, distance, distance + 1, lax.rem(shard + 1, shards))
+
+    def hand_down(group, distance):
+        return hand_on(group, distance, distance - 1, lax.rem(shard + shards - 1, shards))
+
     for group in range(groups):
-        for distance in range(prior, 0, -1):
+        @pl.when(even)
+        def _():
+            hand_up(group, 0).start()
+
+        for distance in reversed(direct):
             @pl.when(shard + distance < shards)
             def _():
                 outer_copy(group, distance).start()
+
+    def relay(group):
+        for distance in direct:
+            @pl.when(shard >= distance)
+            def _():
+                outer_copy(group, distance).wait_recv()
+                if distance < prior:
+                    @pl.when(even)
+                    def _():
+                        hand_up(group, distance).start()
+
+                @pl.when(jnp.logical_not(even))
+                def _():
+                    hand_down(group, distance).start()
 
     for group in range(groups):
         columns = slice(group * HEAD_SIZE, (group + 1) * HEAD_SIZE)
@@ -151,7 +190,8 @@
         for distance in range(1, prior + 1):
             @pl.when(shard >= distance)
             def _():
-                outer_copy(group, distance).wait_recv()
+                if distance % 2:
+                    outer_copy(group, distance).wait_recv()
                 flip(group, prior - distance)
 
         for place in range(prior):
@@ -299,9 +339,17 @@
                 if offset:
                     part_copy(offset, first_row).start()
 
+    relay(0)
     receive(0)
-    tops = lax.fori_loop(0, steps, lambda step, tops: score_step(0, step, tops), lowest)
-
+    half = steps // 2
+    for start in (0, half):
+        if start:
+            relay(1)
+        else:
+            tops = lowest
+        tops = lax.fori_loop(
+            start, start + half, lambda step, tops: score_step(0, step, tops), tops
+        )
     def both_passes(item, tops):
         for group in range(1, groups):
             @pl.when(item == group)
@@ -315,7 +363,15 @@
             totals = value_step(item - 1, step, before, totals)
             return score_step(item, step, now), totals
 
-        tops, totals = lax.fori_loop(0, steps, step_of, (lowest, nothing))
+        def half_of(which, carry):
+            for group in range(2, groups):
+                @pl.when((item == group - 1) & (which == 1))
+                def _():
+                    relay(group)
+
+            return lax.fori_loop(which * half, (which + 1) * half, step_of, carry)
+
+        tops, totals = lax.fori_loop(0, 2, half_of, (lowest, nothing))
         finish_item(item - 1, totals)
         return tops
 
@@ -328,10 +384,25 @@
     finish_item(items - 1, totals)
 
     for group in range(groups):
-        for distance in range(1, prior + 1):
+        @pl.when(even)
+        def _():
+            hand_up(group, 0).wait_send()
+
+        for distance in direct:
             @pl.when(shard + distance < shards)
             def _():
                 outer_copy(group, distance).wait_send()
+
+            @pl.when(shard >= distance)
+            def _():
+                if distance < prior:
+                    @pl.when(even)
+                    def _():
+                        hand_up(group, distance).wait_send()
+
+                @pl.when(jnp.logical_not(even))
+                def _():
+                    hand_down(group, distance).wait_send()
 
     @pl.when(shard + 1 < shards)
     def _():
@@ -394,6 +465,7 @@
             dma(()),
             dma((3,)),
             dma((groups, 2)),
+            dma((groups, prior // 2 + 1)),
         ],
         compiler_params=pltpu.CompilerParams(
             collective_id=0, has_side_effects=True, vmem_limit_bytes=64 * 1024 * 1024 - 2**17

time: 76 us -> 71.8 us (0.945)
  Pallas kernels: 74.1 us -> 70 us
    pallas_call x1, Pallas kernels: 74.1 us -> 70 us  [local(): pl.pallas_call(functools.partial(layer_kernel, shards, owners), out_shape...]
where the time goes in v4:
time: 71.8 us; the launch traced here: 71.7 us
  Pallas kernels  70 us (97%)
  local copies, waits for them, and re-layouts  1.67 us (2%)
    pallas_call x1, Pallas kernels, local(): pl.pallas_call(functools.partial(layer_kernel, shards, owners), out_shape...  70 us
    unnamed x1, local copies, waits for them, and re-layouts  1.67 us

profile of v4, /device:TPU:12, one launch (start us, length us, event | category | flops | bytes accessed | tf_op | source)
XLA Modules:
  0.0 71.7 jit_solution(8450209642719798760)
XLA Ops:
  0.0 70.0 %shard_map.64 = bf16[128,1024]{1,0:T(8,128)(2,1)} custom-call(bf16[128,1024]{1,0:T(8,128)(2,1)} %query_hbm.1, bf16[128,512]{1,0:T(8,128)(2,1)} %key_hbm.1, bf16[128,512]{1,0:T(8,128)(2,1)} %value_hbm.1, bf16[128,512]{1,0:T(8,128)(2,1)} %inner_key_hbm.1, bf16[128,512]{1,0:T(8,128)(2,1)} %inner_value_hbm.1, bf16[1024,4096]{1,0:T(8,128)(2,1)} %weight_hbm.1), custom_call_target="tpu_custom_call" | custom-call | flops 11811160064 | bytes 8388608 | tf_op jit(solution)/shard_map/pallas_call | solution.py:437
  70.0 1.7 %copy.8 = bf16[128,1024]{1,0:T(8,128)(2,1)} copy(bf16[128,1024]{1,0:T(8,128)(2,1)} %shard_map.64) | data formatting | bytes 524288
